TPU v7x, 512 devices: a whole 4x8x8 slice. The times are simulated.
512 devices in a mesh: mem: 128 (over x, z_hi, y, core), tile: 4 (over z_lo).
Axes of the slice: x: 4, y: 8, z: 8 (z_hi: 2, z_lo: 4; z = z_hi * 4 + z_lo), core: 2. Of those that a mesh axis runs over, the one named last changes fastest.
Arguments:
- state: float32 [4, 8, 256, 16, 512], P(None, None, 'mem', 'tile'), may hold values from -5 to 5, as said below
- branch: int32 [16, 512], replicated, may hold values from 0 to 2
- obs_site: int32 [4, 1024], P('tile'), may hold values from 0 to 65535
- obs_value: float32 [4, 1024], P('tile'), may hold values from -6 to 6
- patch_index: int32 [4, 2048, 128], P('tile'), may hold values from 0 to 1023
- patch_weight: float32 [4, 2048, 128], P('tile', 'mem'), may hold values from 0.1 to 4
Outputs:
- analysis: float32 [4, 8, 256, 16, 512], P(None, None, 'mem', 'tile')
Inputs may be any that keep to these rules, and one draw needn't show every extreme that they name: `state`: variable 3 (turbulent kinetic energy) is positive.
All inputs are finite; a program needn't handle non-finite values.
Results may differ from a plain program's by a relative error of at most 0.0003.
Values sent between devices are 32-bit elements; how exact they have to be, the bound alone decides.
A program may use at most 128 MiB of HBM per device.

v0:
```python
import jax
import jax.numpy as jnp
from jax import lax
from jax.experimental import pallas as pl
from jax.experimental.pallas import tpu as pltpu
from jax.sharding import PartitionSpec as P

MESH = pl.DeviceIdType.MESH
F32 = jnp.float32
BF16 = jnp.bfloat16
VMEM = pl.BlockSpec(memory_space=pltpu.VMEM)
ANY = pl.BlockSpec(memory_space=pl.ANY)
LEVELS, ROWS, WIDTH, LANES = 8, 32, 512, 128
MEM, COLS, MEMBERS, PATCH, OBS = 128, 16, 256, 128, 1024


def rem(a, b):
    return lax.rem(a, jnp.int32(b))


def div(a, b):
    return lax.div(a, jnp.int32(b))


def slot_of(device):
    core, y = rem(device, 2), rem(div(device, 2), 8)
    z, x = rem(div(device, 16), 2), div(device, 32)
    return core * 64 + x * 16 + y * 2 + z


def device_at(core, x, y, z):
    return x * 32 + z * 16 + y * 2 + core


def wait_rows(ref, sem, rows):
    part = ref.at[pl.ds(0, rows)]
    pltpu.make_async_copy(part, part, sem).wait()


def send(src, dst, send_sem, recv_sem, mem, tile):
    pltpu.make_async_remote_copy(
        src_ref=src, dst_ref=dst, send_sem=send_sem, recv_sem=recv_sem,
        device_id=(mem, tile), device_id_type=MESH,
    ).start()


def block_transpose(blocks):
    group = lax.broadcasted_iota(jnp.int32, (8, LANES), 1) // 16
    blocks = list(blocks)
    for bit in (1, 2, 4):
        upper = (group // bit) % 2 == 1
        for low in range(8):
            if low & bit:
                continue
            a, b = blocks[low], blocks[low + bit]
            blocks[low] = jnp.where(upper, pltpu.roll(b, 16 * bit, 1), a)
            blocks[low + bit] = jnp.where(upper, b, pltpu.roll(a, LANES - 16 * bit, 1))
    return blocks


def column_step(u, v, theta, energy, stab_m, stab_h):
    n = LEVELS
    km, kh, prod = [], [], []
    for k in range(n - 1):
        scale = 0.6 * jnp.sqrt(0.5 * (energy[k] + energy[k + 1]))
        km.append(scale * stab_m)
        kh.append(scale * stab_h)
        du, dv = u[k + 1] - u[k], v[k + 1] - v[k]
        prod.append(km[k] * (du * du + dv * dv))

    def solve(coef, extra, rhs):
        count = len(rhs)
        ratios, values = [], [[] for _ in range(count)]
        for k in range(n):
            pivot = 1.0 + extra[k] if extra is not None else 1.0
            if k > 0:
                pivot = pivot + coef[k - 1]
            if k < n - 1:
                pivot = pivot + coef[k]
            if k > 0:
                pivot = pivot - coef[k - 1] * ratios[-1]
            inverse = 1.0 / pivot
            for i in range(count):
                top = rhs[i][k]
                if k > 0:
                    top = top + coef[k - 1] * values[i][-1]
                values[i].append(top * inverse)
            if k < n - 1:
                ratios.append(coef[k] * inverse)
        out = []
        for i in range(count):
            result = [values[i][n - 1]]
            for k in range(n - 2, -1, -1):
                result.append(values[i][k] + ratios[k] * result[-1])
            out.append(result[::-1])
        return out

    source = []
    for k in range(n):
        if k == 0:
            total = prod[0]
        elif k == n - 1:
            total = prod[n - 2]
        else:
            total = prod[k - 1] + prod[k]
        source.append(energy[k] + 0.5 * total)
    sink = [0.3 * jnp.sqrt(energy[k]) for k in range(n)]
    new_u, new_v = solve(km, None, [u, v])
    (new_theta,) = solve(kh, None, [theta])
    (new_energy,) = solve(km, sink, [source])
    return new_u, new_v, new_theta, new_energy


def stabilities(branch):
    m = jnp.where(branch == 0, 0.25, jnp.where(branch == 1, 0.6, 1.2)).astype(F32)
    h = jnp.where(branch == 0, 0.15, jnp.where(branch == 1, 0.7, 1.6)).astype(F32)
    return m, h


def mix_columns(src, dst, stab_ref):
    def body(lt, carry):
        base = pl.multiple_of(lt * 256, 256)
        field = [[src[pl.ds(base + (var * 8 + k) * 8, 8), :] for k in range(LEVELS)] for var in range(4)]
        sbase = pl.multiple_of(lt * 16, 16)
        stab_m, stab_h = stab_ref[pl.ds(sbase, 8), :], stab_ref[pl.ds(sbase + 8, 8), :]
        new = column_step(*field, stab_m, stab_h)
        for var in range(4):
            for k in range(LEVELS):
                dst[pl.ds(base + (var * 8 + k) * 8, 8), :] = new[var][k]
        return carry
    lax.fori_loop(0, 4, body, 0)


def rows_of(ref, row):
    return jnp.broadcast_to(ref[pl.ds(row, 1), :], (8, WIDTH))


def laplace_step(centre, up, down):
    total = up + down + pltpu.roll(centre, 1, 1) + pltpu.roll(centre, WIDTH - 1, 1) - 4.0 * centre
    return centre + 0.2 * total


def put_tiles(dst, row, value):
    for lt in range(4):
        dst[pl.ds(pl.multiple_of(lt * 256 + row * 8, 8), 8), :] = value[:, lt * LANES:(lt + 1) * LANES]


def get_tiles(src, row):
    return jnp.concatenate(
        [src[pl.ds(pl.multiple_of(lt * 256 + row * 8, 8), 8), :] for lt in range(4)], axis=1)


def forecast_body(state, branch, stab, stab_edge, to_next, to_prev, from_prev, from_next, mixed, edge, halo_send, halo_recv, me, tile):
    sub = lax.broadcasted_iota(jnp.int32, (8, WIDTH), 0)
    next_tile, prev_tile = rem(tile + 1, 4), rem(tile + 3, 4)

    def pack(row, carry):
        for q, (n_sub, p_sub) in enumerate(((3, 0), (7, 4), (2, 1), (6, 5))):
            to_next[pl.ds(row * 4 + q, 1), :] = state[row, pl.ds(n_sub, 1), :]
            to_prev[pl.ds(row * 4 + q, 1), :] = state[row, pl.ds(p_sub, 1), :]
        return carry
    lax.fori_loop(0, ROWS, pack, 0)
    send(to_next, from_prev, halo_send.at[0], halo_recv.at[0], me, next_tile)
    send(to_prev, from_next, halo_send.at[1], halo_recv.at[1], me, prev_tile)

    own = [rows_of(branch, tile * 4 + x) for x in range(4)]
    before, after = rows_of(branch, rem(tile * 4 + 15, 16)), rows_of(branch, rem(tile * 4 + 4, 16))
    x_of = sub % 4
    own_rows = jnp.where(x_of == 0, own[0], jnp.where(x_of == 1, own[1], jnp.where(x_of == 2, own[2], own[3])))
    edge_rows = jnp.where(x_of < 2, before, after)
    for ref, rows in ((stab, own_rows), (stab_edge, edge_rows)):
        m, h = stabilities(rows)
        for lt in range(4):
            ref[pl.ds(lt * 16, 8), :] = m[:, lt * LANES:(lt + 1) * LANES]
            ref[pl.ds(lt * 16 + 8, 8), :] = h[:, lt * LANES:(lt + 1) * LANES]

    wait_rows(to_next, halo_send.at[0], 128)
    wait_rows(to_prev, halo_send.at[1], 128)
    wait_rows(from_prev, halo_recv.at[0], 128)
    wait_rows(from_next, halo_recv.at[1], 128)

    def pick(a, b, c, d):
        return jnp.where(x_of == 0, a, jnp.where(x_of == 1, b, jnp.where(x_of == 2, c, d)))

    def first(row, carry):
        centre = state[row]
        left = [rows_of(from_prev, row * 4 + q) for q in range(4)]
        right = [rows_of(from_next, row * 4 + q) for q in range(4)]
        up = jnp.where(x_of == 0, jnp.where(sub < 4, left[0], left[1]), pltpu.roll(centre, 1, 0))
        down = jnp.where(x_of == 3, jnp.where(sub < 4, right[0], right[1]), pltpu.roll(centre, 7, 0))
        put_tiles(mixed, row, laplace_step(centre, up, down))
        inner = [jnp.broadcast_to(state[row, pl.ds(s, 1), :], (8, WIDTH)) for s in (0, 4, 3, 7)]
        edge_centre = pick(left[0], left[1], right[0], right[1])
        outer = pick(left[2], left[3], right[2], right[3])
        put_tiles(edge, row, laplace_step(edge_centre, outer, pick(*inner)))
        return carry
    lax.fori_loop(0, ROWS, first, 0)
    mix_columns(mixed, mixed, stab)
    mix_columns(edge, edge, stab_edge)

    def second(row, carry):
        centre = get_tiles(mixed, row)
        sides = get_tiles(edge, row)
        side = [jnp.broadcast_to(sides[q:q + 1, :], (8, WIDTH)) for q in range(4)]
        up = jnp.where(x_of == 0, jnp.where(sub < 4, side[0], side[1]), pltpu.roll(centre, 1, 0))
        down = jnp.where(x_of == 3, jnp.where(sub < 4, side[2], side[3]), pltpu.roll(centre, 7, 0))
        put_tiles(mixed, row, laplace_step(centre, up, down))
        return carry
    lax.fori_loop(0, ROWS, second, 0)
    mix_columns(mixed, mixed, stab)


def observe(mixed, site, obs):
    sub = lax.broadcasted_iota(jnp.int32, (8, LANES), 0)
    sites = site[...]
    lane, x = sites % 128, (sites // 512) % 4
    key = (sites // 2048) * 4 + (sites // 128) % 4

    def spread(a, b):
        return jnp.broadcast_to(a[b:b + 1, :], (8, LANES))
    lanes = [spread(lane, b) for b in range(8)]
    keys = [spread(key, b) for b in range(8)]

    def body(row, accs):
        accs = list(accs)
        for lt in range(4):
            tile = mixed[pl.ds(pl.multiple_of(lt * 256 + row * 8, 8), 8), :]
            for b in range(8):
                found = jnp.take_along_axis(tile, lanes[b], axis=1, mode="promise_in_bounds")
                accs[b] = jnp.where(keys[b] == row * 4 + lt, found, accs[b])
        return tuple(accs)
    accs = lax.fori_loop(0, ROWS, body, tuple(jnp.zeros((8, LANES), F32) for _ in range(8)))
    for b in range(8):
        only = jnp.where(sub % 4 == spread(x, b), accs[b], 0.0)
        only = only + pltpu.roll(only, 7, 0)
        only = only + pltpu.roll(only, 6, 0)
        obs[pl.ds(b, 1), :] = only[0:1, :]
        obs[pl.ds(8 + b, 1), :] = only[4:5, :]


def cut_columns(mixed, tiles):
    def body(n, carry):
        x, lt = div(n, 4), rem(n, 4)
        blocks = [mixed[pl.ds(lt * 256 + var * 64 + m * 4 + x, 8, stride=8), :] for m in range(2) for var in range(4)]
        for g, block in enumerate(block_transpose(blocks)):
            tiles[pl.ds(pl.multiple_of((x * 32 + lt * 8 + g) * 8, 8), 8), :] = block
        return carry
    lax.fori_loop(0, 16, body, 0)


def gather_obs(table, sems, me, tile):
    core, y, z, x = rem(me, 2), rem(div(me, 2), 8), rem(div(me, 16), 2), div(me, 32)
    mine = table.at[pl.ds(pl.multiple_of(slot_of(me) * 16, 16), 16)]
    send(mine, mine, sems.at[0], sems.at[1], device_at(core, x, y, 1 - z), tile)
    yield
    wait_rows(table, sems.at[0], 16)
    wait_rows(table, sems.at[1], 16)
    pair = table.at[pl.ds(pl.multiple_of((core * 64 + x * 16 + y * 2) * 16, 32), 32)]
    for i in range(1, 8):
        send(pair, pair, sems.at[2], sems.at[3], device_at(core, x, rem(y + i, 8), z), tile)
    yield
    wait_rows(table, sems.at[2], 32 * 7)
    wait_rows(table, sems.at[3], 32 * 7)
    plane = table.at[pl.ds(pl.multiple_of((core * 64 + x * 16) * 16, 256), 256)]
    for i in range(1, 4):
        send(plane, plane, sems.at[4], sems.at[5], device_at(core, rem(x + i, 4), y, z), tile)
    yield
    wait_rows(table, sems.at[4], 256 * 3)
    wait_rows(table, sems.at[5], 256 * 3)
    half = table.at[pl.ds(pl.multiple_of(core * 1024, 1024), 1024)]
    send(half, half, sems.at[6], sems.at[7], device_at(1 - core, x, y, z), tile)
    yield
    wait_rows(table, sems.at[6], 1024)
    wait_rows(table, sems.at[7], 1024)


def greet(me, tile, with_tiles):
    barrier = pltpu.get_barrier_semaphore()
    count = MEM - 1
    if with_tiles:
        for step in (1, 3):
            pl.semaphore_signal(barrier, inc=1, device_id=(me, rem(tile + step, 4)), device_id_type=MESH)
        count += 2

    def body(i, carry):
        pl.semaphore_signal(barrier, inc=1, device_id=(rem(me + i, MEM), tile), device_id_type=MESH)
        return carry
    lax.fori_loop(1, MEM, body, 0)
    pl.semaphore_wait(barrier, count)


def forecast_kernel(state, branch, site, columns, table,
                    stab, stab_edge, to_next, to_prev, from_prev, from_next, mixed, edge, tiles, obs,
                    halo_send, halo_recv, gather_sems, out_sem, in_sem, own_sem):
    me, tile = lax.axis_index("mem"), lax.axis_index("tile")
    greet(me, tile, True)
    forecast_body(state, branch, stab, stab_edge, to_next, to_prev, from_prev, from_next, mixed, edge, halo_send, halo_recv, me, tile)
    observe(mixed, site, obs)
    slot = slot_of(me)
    table[pl.ds(pl.multiple_of(slot * 16, 16), 16), :] = obs[...]
    gather = gather_obs(table, gather_sems, me, tile)
    next(gather)
    cut_columns(mixed, tiles)
    next(gather)
    next(gather)
    here = pl.ds(pl.multiple_of(slot * 8, 8), 8)

    def body(i, carry):
        to = rem(me + i, MEM)
        send(tiles.at[pl.ds(pl.multiple_of(to * 8, 8), 8)], columns.at[here], out_sem, in_sem, to, tile)
        return carry
    lax.fori_loop(1, MEM, body, 0)
    columns[here, :] = tiles[pl.ds(pl.multiple_of(me * 8, 8), 8), :]
    next(gather)
    for _ in gather:
        pass
    wait_rows(tiles, out_sem, 8 * (MEM - 1))
    wait_rows(columns, in_sem, 8 * (MEM - 1))


def split(a):
    high = a.astype(BF16)
    return high, (a - high.astype(F32)).astype(BF16)


def dot(a, b):
    return jnp.dot(a, b, preferred_element_type=F32)


def dot_t(a, b):
    return lax.dot_general(a, b, (((1,), (1,)), ((), ())), preferred_element_type=F32)


def dot3(a, pair):
    high, low = split(a)
    return dot(high, pair[0]) + (dot(low, pair[0]) + dot(high, pair[1]))


def prepare(columns, table, value, index, weight, fields, lookup, turned, gap):
    total = table[pl.ds(0, 16), :]
    total = lax.fori_loop(1, MEM, lambda s, t: t + table[pl.ds(pl.multiple_of(s * 16, 16), 16), :], total)
    mean = (total[:8] + total[8:]) * (1.0 / MEMBERS)
    diff = value[...] - mean
    for b in range(8):
        for m in range(2):
            block = table[pl.ds(m * 8 + b, MEM, stride=16), :] - mean[b:b + 1, :]
            high, low = split(jnp.transpose(block))
            lookup[pl.ds(b * 128, 128), pl.ds(m * 128, 128)] = high
            lookup[pl.ds(b * 128, 128), pl.ds(256 + m * 128, 128)] = low
    for level in range(LEVELS):
        fields[pl.ds(level * 128, 128), :] = jnp.transpose(columns[pl.ds(level, MEM, stride=8), :])
    indices = index[...]
    both = jnp.concatenate([indices.astype(F32), weight[...], jnp.zeros((96, LANES), F32)], axis=0)
    turned[...] = jnp.transpose(both)
    for part in range(2):
        own = indices[part * 8:part * 8 + 8]
        found = jnp.zeros((8, LANES), F32)
        for b in range(8):
            row = jnp.broadcast_to(diff[b:b + 1, :], (8, LANES))
            taken = jnp.take_along_axis(row, own % 128, axis=1, mode="promise_in_bounds")
            found = jnp.where(own // 128 == b, taken, found)
        gap[pl.ds(part * 8, 8), :] = found


def one_column(c, index_col, weight_col, weight, fields, lookup, gap, analysed):
    eye = (lax.broadcasted_iota(jnp.int32, (PATCH, PATCH), 0) == lax.broadcasted_iota(jnp.int32, (PATCH, PATCH), 1)).astype(F32)
    places = lax.broadcasted_iota(jnp.int32, (PATCH, OBS), 1)
    chosen = (places == index_col.astype(jnp.int32)).astype(F32).astype(BF16)
    picked = dot(chosen, lookup[...])
    high, low = picked[:, :MEMBERS].astype(BF16), picked[:, MEMBERS:].astype(BF16)
    rows = [(m * 4 + var) * 16 + c for m in range(2) for var in range(4)]
    parts = [fields[pl.ds(r, 8, stride=128), :] for r in rows]
    x = jnp.concatenate([jnp.concatenate(parts[:4], axis=0), jnp.concatenate(parts[4:], axis=0)], axis=1)
    mean = jnp.sum(x, axis=1, keepdims=True) * (1.0 / MEMBERS)
    pert = x - mean
    pert_high, pert_low = split(pert)
    top, bottom = jnp.concatenate([high, pert_high], axis=0), jnp.concatenate([low, pert_low], axis=0)
    products = dot_t(top, high) + (dot_t(top, low) + dot_t(bottom, high))
    w = weight[pl.ds(c, 1), :]
    cov = products[:PATCH]
    cov_w = cov * (w * (1.0 / (MEMBERS - 1.0)))
    cross_w = products[PATCH:] * (w * (1.0 / (MEMBERS - 1.0)))
    trace = jnp.sum(cov_w * eye, keepdims=True)
    square = jnp.sum(cov_w * cov * (weight_col * (1.0 / (MEMBERS - 1.0))), keepdims=True)
    norm = jnp.sqrt(MEMBERS + 2.0 * trace + square)
    inv = 1.0 / norm
    step = (eye + cov_w) * inv
    step_pair = split(step)
    cross = jnp.concatenate([cross_w * inv, jnp.zeros((8, PATCH), F32)], axis=0)
    first_row = lax.broadcasted_iota(jnp.int32, (8, PATCH), 0) == 0
    force = jnp.where(first_row, w * gap[pl.ds(c, 1), :], 0.0)
    square_step = dot3(step, step_pair)
    inner = 2.25 * eye - 1.5 * step + 0.25 * square_step
    turn_pair = split(dot3(inner, step_pair))
    rate = 1.5 - 0.5 * inv
    start = dot3(jnp.concatenate([cross[:ROWS], force], axis=0), step_pair)
    zero8 = jnp.zeros((8, PATCH), F32)
    v = 1.5 * cross[:ROWS] - 0.5 * (start[:ROWS] + inv * cross[:ROWS])
    a_v = inv * rate
    v = 1.5 * v - 0.5 * (dot3(v, step_pair) + a_v * cross[:ROWS])
    t1 = a_v * rate
    v = jnp.concatenate([v, zero8], axis=0)
    u = jnp.concatenate([-0.5 * cross[:ROWS], 1.5 * force - 0.5 * start[ROWS:]], axis=0)
    a = rate

    def times_t1(a, u):
        return a * t1, dot3(u, turn_pair) + a * v

    def times_f1(a, u):
        a2, u2 = times_t1(a, u)
        return 1.5 * a - 0.5 * a2, 1.5 * u - 0.5 * u2
    a, u = times_f1(a, u)
    a2, u2 = times_f1(*times_f1(*times_t1(a, u)))
    a, u = 1.5 * a - 0.5 * a2, 1.5 * u - 0.5 * u2
    spread = dot3(u, (high, low))
    scale = 1.0 / jnp.sqrt(norm)
    moved = (a * pert + spread[:ROWS]) * scale
    nudge = spread[ROWS:ROWS + 1] * scale
    centre = mean + jnp.sum(moved * nudge, axis=1, keepdims=True) * (1.0 / (MEMBERS - 1.0))
    out = moved + centre
    for m in range(2):
        for var in range(4):
            analysed[pl.ds((m * 4 + var) * 16 + c, 8, stride=128), :] = out[var * 8:var * 8 + 8, m * 128:m * 128 + 128]


UNROLL = 2


def analysis_kernel(columns, table, value, index_all, weight, outgoing, index, fields, lookup, turned, gap, analysed, sem):
    me = lax.axis_index("mem")
    copy = pltpu.make_async_copy(index_all.at[0, pl.ds(pl.multiple_of(me * COLS, COLS), COLS)], index, sem)
    copy.start()
    copy.wait()
    prepare(columns, table, value, index, weight, fields, lookup, turned, gap)

    def body(n, carry):
        here = pltpu.roll(turned[...], LANES - n * UNROLL, 1)
        for i in range(UNROLL):
            one_column(n * UNROLL + i, here[:, i:i + 1], here[:, COLS + i:COLS + i + 1], weight, fields, lookup, gap, analysed)
        return carry
    lax.fori_loop(0, COLS // UNROLL, body, 0)
    for level in range(LEVELS):
        outgoing[pl.ds(level, MEM, stride=8), :] = jnp.transpose(analysed[pl.ds(level * 128, 128), :])


def return_kernel(outgoing, result, landed, out_sem, in_sem):
    me, tile = lax.axis_index("mem"), lax.axis_index("tile")
    greet(me, tile, False)
    here = pl.ds(pl.multiple_of(me * 8, 8), 8)

    def body(i, carry):
        to = rem(me + i, MEM)
        send(outgoing.at[pl.ds(pl.multiple_of(slot_of(to) * 8, 8), 8)], landed.at[here], out_sem, in_sem, to, tile)
        return carry
    lax.fori_loop(1, MEM, body, 0)
    landed[here, :] = outgoing[pl.ds(pl.multiple_of(slot_of(me) * 8, 8), 8), :]
    wait_rows(outgoing, out_sem, 8 * (MEM - 1))
    wait_rows(landed, in_sem, 8 * (MEM - 1))
    place(landed, result)


def place(landed, result):
    def body(n, carry):
        x, lt = div(n, 4), rem(n, 4)
        blocks = [landed[pl.ds(pl.multiple_of((x * 32 + lt * 8 + g) * 8, 8), 8), :] for g in range(8)]
        blocks = block_transpose(blocks)
        for m in range(2):
            for var in range(4):
                result[pl.ds(lt * 256 + var * 64 + m * 4 + x, 8, stride=8), :] = blocks[m * 4 + var]
        return carry
    lax.fori_loop(0, 16, body, 0)


def shape(*dims, dtype=F32):
    return jax.ShapeDtypeStruct(dims, dtype)


def per_device(state, branch, obs_site, obs_value, patch_index, patch_weight):
    fields = state.reshape(ROWS, 8, WIDTH)
    dma = pltpu.SemaphoreType.DMA
    columns, table = pl.pallas_call(
        forecast_kernel,
        name="forecast",
        out_shape=[shape(MEM * 8, LANES), shape(MEM * 16, LANES)],
        in_specs=[VMEM] * 3,
        out_specs=[VMEM] * 2,
        scratch_shapes=[
            pltpu.VMEM((64, LANES), F32), pltpu.VMEM((64, LANES), F32),
            pltpu.VMEM((128, WIDTH), F32), pltpu.VMEM((128, WIDTH), F32),
            pltpu.VMEM((128, WIDTH), F32), pltpu.VMEM((128, WIDTH), F32),
            pltpu.VMEM((1024, LANES), F32), pltpu.VMEM((1024, LANES), F32), pltpu.VMEM((1024, LANES), F32),
            pltpu.VMEM((16, LANES), F32),
            dma((2,)), dma((2,)), dma((8,)), dma(()), dma(()), dma(()),
        ],
        compiler_params=pltpu.CompilerParams(collective_id=1, has_side_effects=True, vmem_limit_bytes=32 * 1024 * 1024),
    )(fields, branch, obs_site.reshape(8, LANES))
    outgoing = pl.pallas_call(
        analysis_kernel,
        name="analysis",
        out_shape=shape(MEM * 8, LANES),
        in_specs=[VMEM, VMEM, VMEM, ANY, VMEM],
        out_specs=VMEM,
        scratch_shapes=[
            pltpu.VMEM((COLS, LANES), jnp.int32), pltpu.VMEM((1024, LANES), F32), pltpu.VMEM((OBS, 2 * MEMBERS), BF16),
            pltpu.VMEM((LANES, LANES), F32), pltpu.VMEM((COLS, LANES), F32), pltpu.VMEM((1024, LANES), F32), dma(()),
        ],
        compiler_params=pltpu.CompilerParams(vmem_limit_bytes=32 * 1024 * 1024),
    )(columns, table, obs_value.reshape(8, LANES), patch_index, patch_weight.reshape(COLS, LANES))
    result = pl.pallas_call(
        return_kernel,
        name="return",
        out_shape=shape(1024, LANES),
        in_specs=[VMEM],
        out_specs=VMEM,
        scratch_shapes=[pltpu.VMEM((1024, LANES), F32), dma(()), dma(())],
        compiler_params=pltpu.CompilerParams(collective_id=2, has_side_effects=True, vmem_limit_bytes=32 * 1024 * 1024),
    )(outgoing)
    return result.reshape(4, ROWS, 2, 4, LANES).transpose(1, 2, 3, 0, 4).reshape(state.shape)


def solution(mesh):
    placed = (
        P(None, None, "mem", "tile", None),
        P(),
        P("tile", None),
        P("tile", None),
        P("tile", None, None),
        P("tile", "mem", None),
    )
    return jax.shard_map(
        per_device,
        mesh=mesh,
        in_specs=placed,
        out_specs=P(None, None, "mem", "tile", None),
        check_vma=False,
    )
```

profile of v0, /device:TPU:1, one launch (start us, length us, event | category | flops | bytes accessed | tf_op | source)
XLA Modules:
  0.0 133.2 jit_solution(8950644548870648064)
XLA Ops:
  0.0 0.0 copy-start
  0.0 0.0 copy-start.3
  0.0 1.3 reshape.18.state
  1.3 0.0 copy-done.3
  1.3 0.0 copy-start.1
  1.4 0.7 copy-done.1
  2.1 0.0 copy-start.2
  2.1 0.0 copy-start.4
  2.1 69.8 %forecast.1 = (f32[1024,128]{1,0:T(8,128)S(1)}, f32[2048,128]{1,0:T(8,128)S(1)}) custom-call(f32[32,8,512]{2,1,0:T(8,128)S(1)} %reshape.18.state, s32[16,512]{1,0:T(8,128)S(1)} %copy-done.1, s32[8,128]{1,0:T(8,128)S(1)} %bitcast.8), custom_call_target="tpu_custom_call" | custom-call | tf_op jit(solution)/shard_map/forecast/pallas_call | solution.py:481
  71.9 0.0 copy-done
  72.0 0.0 copy-done.2
  72.0 0.0 copy-done.4
  72.0 31.2 %analysis.1.outgoing = f32[1024,128]{1,0:T(8,128)S(1)} custom-call(f32[1024,128]{1,0:T(8,128)S(1)} %get-tuple-element.7.columns, f32[2048,128]{1,0:T(8,128)S(1)} %get-tuple-element.8.table, f32[8,128]{1,0:T(8,128)S(1)} %bitcast.9, s32[1,2048,128]{2,1,0:T(8,128)S(1)} %copy-done, f32[16,128]{1,0:T(8,128)S(1)} %bitcast.7), custom_call_target="tpu_custom_call" | custom-call | tf_op jit(solution)/shard_map/analysis/pallas_call | solution.py:497
  103.2 28.6 %return.1 = f32[1024,128]{1,0:T(8,128)S(1)} custom-call(f32[1024,128]{1,0:T(8,128)S(1)} %analysis.1.outgoing), custom_call_target="tpu_custom_call" | custom-call | tf_op jit(solution)/shard_map/return/pallas_call | solution.py:509
  131.8 0.3 copy.7
  132.1 1.1 reshape.23
Async XLA Ops:
  0.0 72.0 %copy-start = (s32[1,2048,128]{2,1,0:T(8,128)S(1)}, s32[1,2048,128]{2,1,0:T(8,128)}, u32[]{:S(2)}) copy-start(s32[1,2048,128]{2,1,0:T(8,128)} %index_all.1) | copy-start | bytes 3145732
  0.0 1.3 copy-start.3
  1.3 0.8 copy-start.1
  2.1 69.9 %copy-start.2 = (f32[1,16,128]{2,1,0:T(8,128)S(1)}, f32[1,16,128]{2,1,0:T(8,128)}, u32[]{:S(2)}) copy-start(f32[1,16,128]{2,1,0:T(8,128)} %param.11) | copy-start | bytes 24580
  2.1 69.9 %copy-start.4 = (f32[1,1024]{1,0:T(1,128)S(1)}, f32[1,1024]{1,0:T(1,128)}, u32[]{:S(2)}) copy-start(f32[1,1024]{1,0:T(1,128)} %param.9) | copy-start | bytes 12292
where the time goes:
time: 133 us
  Pallas kernels  130 us (98%)
  local copies, waits for them, and re-layouts  3.53 us (3%)
    pallas_call x1, Pallas kernels, per_device(): pl.pallas_call(forecast_kernel, name='forecast', out_shape=[shape(MEM * 8...  69.8 us
    pallas_call x1, Pallas kernels, per_device(): pl.pallas_call(analysis_kernel, name='analysis', out_shape=shape(MEM * 8,...  31.2 us
    pallas_call x1, Pallas kernels, per_device(): pl.pallas_call(return_kernel, name='return', out_shape=shape(1024, LANES)...  28.6 us

commit v1 on v0

v1 whole, which is shorter than its diff:
```python
import jax
import jax.numpy as jnp
from jax import lax
from jax.experimental import pallas as pl
from jax.experimental.pallas import tpu as pltpu
from jax.sharding import PartitionSpec as P

MESH = pl.DeviceIdType.MESH
F32 = jnp.float32
BF16 = jnp.bfloat16
VMEM = pl.BlockSpec(memory_space=pltpu.VMEM)
ANY = pl.BlockSpec(memory_space=pl.ANY)
LEVELS, ROWS, WIDTH, LANES = 8, 32, 512, 128
MEM, COLS, MEMBERS, PATCH, OBS = 128, 16, 256, 128, 1024


def rem(a, b):
    return lax.rem(a, jnp.int32(b))


def div(a, b):
    return lax.div(a, jnp.int32(b))


def slot_of(device):
    core, y = rem(device, 2), rem(div(device, 2), 8)
    z, x = rem(div(device, 16), 2), div(device, 32)
    return core * 64 + x * 16 + y * 2 + z


def device_at(core, x, y, z):
    return x * 32 + z * 16 + y * 2 + core


def wait_rows(ref, sem, rows):
    part = ref.at[pl.ds(0, rows)]
    pltpu.make_async_copy(part, part, sem).wait()


def send(src, dst, send_sem, recv_sem, mem, tile):
    pltpu.make_async_remote_copy(
        src_ref=src, dst_ref=dst, send_sem=send_sem, recv_sem=recv_sem,
        device_id=(mem, tile), device_id_type=MESH,
    ).start()


def block_transpose(blocks):
    group = lax.broadcasted_iota(jnp.int32, (8, LANES), 1) // 16
    blocks = list(blocks)
    for bit in (1, 2, 4):
        upper = (group // bit) % 2 == 1
        for low in range(8):
            if low & bit:
                continue
            a, b = blocks[low], blocks[low + bit]
            blocks[low] = jnp.where(upper, pltpu.roll(b, 16 * bit, 1), a)
            blocks[low + bit] = jnp.where(upper, b, pltpu.roll(a, LANES - 16 * bit, 1))
    return blocks


def column_step(u, v, theta, energy, stab_m, stab_h):
    n = LEVELS
    km, kh, prod = [], [], []
    for k in range(n - 1):
        scale = 0.6 * jnp.sqrt(0.5 * (energy[k] + energy[k + 1]))
        km.append(scale * stab_m)
        kh.append(scale * stab_h)
        du, dv = u[k + 1] - u[k], v[k + 1] - v[k]
        prod.append(km[k] * (du * du + dv * dv))

    def solve(coef, extra, rhs):
        count = len(rhs)
        ratios, values = [], [[] for _ in range(count)]
        for k in range(n):
            pivot = 1.0 + extra[k] if extra is not None else 1.0
            if k > 0:
                pivot = pivot + coef[k - 1]
            if k < n - 1:
                pivot = pivot + coef[k]
            if k > 0:
                pivot = pivot - coef[k - 1] * ratios[-1]
            inverse = 1.0 / pivot
            for i in range(count):
                top = rhs[i][k]
                if k > 0:
                    top = top + coef[k - 1] * values[i][-1]
                values[i].append(top * inverse)
            if k < n - 1:
                ratios.append(coef[k] * inverse)
        out = []
        for i in range(count):
            result = [values[i][n - 1]]
            for k in range(n - 2, -1, -1):
                result.append(values[i][k] + ratios[k] * result[-1])
            out.append(result[::-1])
        return out

    source = []
    for k in range(n):
        if k == 0:
            total = prod[0]
        elif k == n - 1:
            total = prod[n - 2]
        else:
            total = prod[k - 1] + prod[k]
        source.append(energy[k] + 0.5 * total)
    sink = [0.3 * jnp.sqrt(energy[k]) for k in range(n)]
    new_u, new_v = solve(km, None, [u, v])
    (new_theta,) = solve(kh, None, [theta])
    (new_energy,) = solve(km, sink, [source])
    return new_u, new_v, new_theta, new_energy


def stabilities(branch):
    m = jnp.where(branch == 0, 0.25, jnp.where(branch == 1, 0.6, 1.2)).astype(F32)
    h = jnp.where(branch == 0, 0.15, jnp.where(branch == 1, 0.7, 1.6)).astype(F32)
    return m, h


def mix_columns(src, dst, stab_ref):
    def body(lt, carry):
        base = pl.multiple_of(lt * 256, 256)
        field = [[src[pl.ds(base + (var * 8 + k) * 8, 8), :] for k in range(LEVELS)] for var in range(4)]
        sbase = pl.multiple_of(lt * 16, 16)
        stab_m, stab_h = stab_ref[pl.ds(sbase, 8), :], stab_ref[pl.ds(sbase + 8, 8), :]
        new = column_step(*field, stab_m, stab_h)
        for var in range(4):
            for k in range(LEVELS):
                dst[pl.ds(base + (var * 8 + k) * 8, 8), :] = new[var][k]
        return carry
    lax.fori_loop(0, 4, body, 0)


def rows_of(ref, row):
    return jnp.broadcast_to(ref[pl.ds(row, 1), :], (8, WIDTH))


def laplace_step(centre, up, down):
    total = up + down + pltpu.roll(centre, 1, 1) + pltpu.roll(centre, WIDTH - 1, 1) - 4.0 * centre
    return centre + 0.2 * total


def put_tiles(dst, row, value):
    for lt in range(4):
        dst[pl.ds(pl.multiple_of(lt * 256 + row * 8, 8), 8), :] = value[:, lt * LANES:(lt + 1) * LANES]


def get_tiles(src, row):
    return jnp.concatenate(
        [src[pl.ds(pl.multiple_of(lt * 256 + row * 8, 8), 8), :] for lt in range(4)], axis=1)


def forecast_body(state, branch, stab, stab_edge, to_next, to_prev, from_prev, from_next, mixed, edge, halo_send, halo_recv, me, tile, rounds):
    sub = lax.broadcasted_iota(jnp.int32, (8, WIDTH), 0)
    next_tile, prev_tile = rem(tile + 1, 4), rem(tile + 3, 4)

    def pack(row, carry):
        for q, (n_sub, p_sub) in enumerate(((3, 0), (7, 4), (2, 1), (6, 5))):
            to_next[pl.ds(row * 4 + q, 1), :] = state[row, pl.ds(n_sub, 1), :]
            to_prev[pl.ds(row * 4 + q, 1), :] = state[row, pl.ds(p_sub, 1), :]
        return carry
    lax.fori_loop(0, ROWS, pack, 0)
    send(to_next, from_prev, halo_send.at[0], halo_recv.at[0], me, next_tile)
    send(to_prev, from_next, halo_send.at[1], halo_recv.at[1], me, prev_tile)

    own = [rows_of(branch, tile * 4 + x) for x in range(4)]
    before, after = rows_of(branch, rem(tile * 4 + 15, 16)), rows_of(branch, rem(tile * 4 + 4, 16))
    x_of = sub % 4
    own_rows = jnp.where(x_of == 0, own[0], jnp.where(x_of == 1, own[1], jnp.where(x_of == 2, own[2], own[3])))
    edge_rows = jnp.where(x_of < 2, before, after)
    for ref, rows in ((stab, own_rows), (stab_edge, edge_rows)):
        m, h = stabilities(rows)
        for lt in range(4):
            ref[pl.ds(lt * 16, 8), :] = m[:, lt * LANES:(lt + 1) * LANES]
            ref[pl.ds(lt * 16 + 8, 8), :] = h[:, lt * LANES:(lt + 1) * LANES]

    next(rounds)
    wait_rows(to_next, halo_send.at[0], 128)
    wait_rows(to_prev, halo_send.at[1], 128)
    wait_rows(from_prev, halo_recv.at[0], 128)
    wait_rows(from_next, halo_recv.at[1], 128)
    next(rounds)

    def pick(a, b, c, d):
        return jnp.where(x_of == 0, a, jnp.where(x_of == 1, b, jnp.where(x_of == 2, c, d)))

    def first(row, carry):
        centre = state[row]
        left = [rows_of(from_prev, row * 4 + q) for q in range(4)]
        right = [rows_of(from_next, row * 4 + q) for q in range(4)]
        up = jnp.where(x_of == 0, jnp.where(sub < 4, left[0], left[1]), pltpu.roll(centre, 1, 0))
        down = jnp.where(x_of == 3, jnp.where(sub < 4, right[0], right[1]), pltpu.roll(centre, 7, 0))
        put_tiles(mixed, row, laplace_step(centre, up, down))
        inner = [jnp.broadcast_to(state[row, pl.ds(s, 1), :], (8, WIDTH)) for s in (0, 4, 3, 7)]
        edge_centre = pick(left[0], left[1], right[0], right[1])
        outer = pick(left[2], left[3], right[2], right[3])
        put_tiles(edge, row, laplace_step(edge_centre, outer, pick(*inner)))
        return carry
    lax.fori_loop(0, ROWS, first, 0, unroll=4)
    mix_columns(mixed, mixed, stab)
    mix_columns(edge, edge, stab_edge)
    next(rounds)

    def second(row, carry):
        centre = get_tiles(mixed, row)
        sides = get_tiles(edge, row)
        side = [jnp.broadcast_to(sides[q:q + 1, :], (8, WIDTH)) for q in range(4)]
        up = jnp.where(x_of == 0, jnp.where(sub < 4, side[0], side[1]), pltpu.roll(centre, 1, 0))
        down = jnp.where(x_of == 3, jnp.where(sub < 4, side[2], side[3]), pltpu.roll(centre, 7, 0))
        put_tiles(mixed, row, laplace_step(centre, up, down))
        return carry
    lax.fori_loop(0, ROWS, second, 0, unroll=4)
    mix_columns(mixed, mixed, stab)


def observe(mixed, site, obs):
    sub = lax.broadcasted_iota(jnp.int32, (8, LANES), 0)
    sites = site[...]
    lane, x = sites % 128, (sites // 512) % 4
    key = (sites // 2048) * 4 + (sites // 128) % 4

    def spread(a, b):
        return jnp.broadcast_to(a[b:b + 1, :], (8, LANES))
    lanes = [spread(lane, b) for b in range(8)]
    keys = [spread(key, b) for b in range(8)]

    accs = []
    for b in range(8):
        def body(row, acc):
            for lt in range(4):
                tile = mixed[pl.ds(pl.multiple_of(lt * 256 + row * 8, 8), 8), :]
                found = jnp.take_along_axis(tile, lanes[b], axis=1, mode="promise_in_bounds")
                acc = jnp.where(keys[b] == row * 4 + lt, found, acc)
            return acc
        accs.append(lax.fori_loop(0, ROWS, body, jnp.zeros((8, LANES), F32), unroll=8))
    for b in range(8):
        only = jnp.where(sub % 4 == spread(x, b), accs[b], 0.0)
        only = only + pltpu.roll(only, 7, 0)
        only = only + pltpu.roll(only, 6, 0)
        obs[pl.ds(b, 1), :] = only[0:1, :]
        obs[pl.ds(8 + b, 1), :] = only[4:5, :]


def cut_columns(mixed, tiles):
    def body(n, carry):
        x, lt = div(n, 4), rem(n, 4)
        blocks = [mixed[pl.ds(lt * 256 + var * 64 + m * 4 + x, 8, stride=8), :] for m in range(2) for var in range(4)]
        for g, block in enumerate(block_transpose(blocks)):
            tiles[pl.ds(pl.multiple_of((x * 32 + lt * 8 + g) * 8, 8), 8), :] = block
        return carry
    lax.fori_loop(0, 16, body, 0, unroll=4)


def gather_obs(table, sems, me, tile):
    core, y, x = rem(me, 2), rem(div(me, 2), 8), div(me, 32)
    starts = (slot_of(me), core * 64 + x * 16 + y * 2, core * 64 + x * 16, core * 64)
    for n, (group, start, count) in enumerate(zip(near(me), starts, (1, 2, 16, 64))):
        rows = count * 16
        block = table.at[pl.ds(pl.multiple_of(start * 16, rows), rows)]
        for to in group:
            send(block, block, sems.at[2 * n], sems.at[2 * n + 1], to, tile)
        yield
        wait_rows(table, sems.at[2 * n], rows * len(group))
        wait_rows(table, sems.at[2 * n + 1], rows * len(group))


def near(me):
    core, y, z, x = rem(me, 2), rem(div(me, 2), 8), rem(div(me, 16), 2), div(me, 32)
    return (
        [device_at(core, x, y, 1 - z)],
        [device_at(core, x, rem(y + i, 8), z) for i in range(1, 8)],
        [device_at(core, rem(x + i, 4), y, z) for i in range(1, 4)],
        [device_at(1 - core, x, y, z)],
    )


def greet(me, tile):
    barrier = pltpu.get_barrier_semaphore()
    for step in (1, 3):
        pl.semaphore_signal(barrier, inc=1, device_id=(me, rem(tile + step, 4)), device_id_type=MESH)
    for group in near(me):
        for to in group:
            pl.semaphore_signal(barrier, inc=1, device_id=(to, tile), device_id_type=MESH)
    pl.semaphore_wait(barrier, 14)


def pass_on(arrived, me, tile):
    for n, group in enumerate(near(me)):
        for to in group:
            pl.semaphore_signal(arrived.at[n], inc=1, device_id=(to, tile), device_id_type=MESH)
        yield
        pl.semaphore_wait(arrived.at[n], len(group))


def split(a):
    high = a.astype(BF16)
    return high, (a - high.astype(F32)).astype(BF16)


def dot(a, b):
    return jnp.dot(a, b, preferred_element_type=F32)


def dot_t(a, b):
    return lax.dot_general(a, b, (((1,), (1,)), ((), ())), preferred_element_type=F32)


def dot3(a, pair):
    high, low = split(a)
    return dot(high, pair[0]) + (dot(low, pair[0]) + dot(high, pair[1]))


def prepare(table, value, index, weight, lookup, turned, gap):
    total = table[pl.ds(0, 16), :]
    total = lax.fori_loop(1, MEM, lambda s, t: t + table[pl.ds(pl.multiple_of(s * 16, 16), 16), :], total)
    mean = (total[:8] + total[8:]) * (1.0 / MEMBERS)
    diff = value[...] - mean
    for b in range(8):
        for m in range(2):
            block = table[pl.ds(m * 8 + b, MEM, stride=16), :] - mean[b:b + 1, :]
            high, low = split(jnp.transpose(block))
            lookup[pl.ds(b * 128, 128), pl.ds(m * 128, 128)] = high
            lookup[pl.ds(b * 128, 128), pl.ds(256 + m * 128, 128)] = low
    indices = index[...]
    both = jnp.concatenate([indices.astype(F32), weight[...], jnp.zeros((96, LANES), F32)], axis=0)
    turned[...] = jnp.transpose(both)
    for part in range(2):
        own = indices[part * 8:part * 8 + 8]
        found = jnp.zeros((8, LANES), F32)
        for b in range(8):
            row = jnp.broadcast_to(diff[b:b + 1, :], (8, LANES))
            taken = jnp.take_along_axis(row, own % 128, axis=1, mode="promise_in_bounds")
            found = jnp.where(own // 128 == b, taken, found)
        gap[pl.ds(part * 8, 8), :] = found


def eye():
    shape = (PATCH, PATCH)
    return (lax.broadcasted_iota(jnp.int32, shape, 0) == lax.broadcasted_iota(jnp.int32, shape, 1)).astype(F32)


def stacked(a):
    return jnp.concatenate(split(a), axis=0)


def beside(a):
    return jnp.concatenate(split(a), axis=1)


def folded(p, rows, width):
    return (p[:rows, :width] + p[rows:, :width]) + (p[:rows, width:] + p[rows:, width:])


GROUP = 4
BATCH = 4


def pick_obs(turned, lookup, picked):
    places = lax.broadcasted_iota(jnp.int32, (PATCH, OBS), 1)

    def body(n, carry):
        here = pltpu.roll(turned[...], LANES - n * GROUP, 1)
        chosen = [(places == here[:, i:i + 1].astype(jnp.int32)).astype(F32).astype(BF16) for i in range(GROUP)]
        rows = GROUP * PATCH
        found = dot(jnp.concatenate(chosen, axis=0), lookup[...])
        picked[pl.ds(pl.multiple_of(n * rows, rows), rows), :] = found.astype(BF16)
        return carry
    lax.fori_loop(0, COLS // GROUP, body, 0)


def patch_of(picked, c):
    return picked[pl.ds(pl.multiple_of(c * PATCH, PATCH), PATCH), :]


def sweep(turned, weight, picked, steps, turns, norms):
    def body(n, carry):
        one = eye()
        here = pltpu.roll(turned[...], LANES - n * BATCH, 1)
        cs = [n * BATCH + i for i in range(BATCH)]
        both = [patch_of(picked, c) for c in cs]
        both = [jnp.concatenate([p[:, :MEMBERS], p[:, MEMBERS:]], axis=0) for p in both]
        cov = [folded(dot_t(q, q), PATCH, PATCH) for q in both]
        cov_w = [v * (weight[pl.ds(c, 1), :] * (1.0 / (MEMBERS - 1.0))) for v, c in zip(cov, cs)]
        inv = []
        for i in range(BATCH):
            column = here[:, COLS + i:COLS + i + 1] * (1.0 / (MEMBERS - 1.0))
            total = jnp.sum(cov_w[i] * (2.0 * one + cov[i] * column), axis=0, keepdims=True)
            total = jnp.sum(total, axis=1, keepdims=True)
            inv.append(jnp.broadcast_to(1.0 / jnp.sqrt(MEMBERS + total), (1, PATCH)))
        step = [(one + v) * t for v, t in zip(cov_w, inv)]
        parts = [split(k) for k in step]
        wide = [jnp.concatenate(p, axis=1) for p in parts]
        square = [folded(dot(jnp.concatenate(p, axis=0), k), PATCH, PATCH) for p, k in zip(parts, wide)]
        inner = [2.25 * one - 1.5 * k + 0.25 * q for k, q in zip(step, square)]
        turn = [folded(dot(stacked(g), k), PATCH, PATCH) for g, k in zip(inner, wide)]
        for i, c in enumerate(cs):
            here_rows = pl.ds(pl.multiple_of(c * PATCH, PATCH), PATCH)
            steps[here_rows, :] = wide[i]
            turns[here_rows, :] = beside(turn[i])
            norms[pl.ds(c, 1), :] = inv[i]
        return carry
    lax.fori_loop(0, COLS // BATCH, body, 0)


def apply(fields, weight, gap, picked, steps, turns, norms, analysed):
    def body(n, carry):
        cs = [n * BATCH + i for i in range(BATCH)]
        todo = range(BATCH)
        first_row = lax.broadcasted_iota(jnp.int32, (16, PATCH), 0) == 0
        zeros = jnp.zeros((16, PATCH), F32)
        x = []
        for c in cs:
            parts = [fields[pl.ds((m * 4 + var) * 16 + c, 8, stride=128), :] for m in range(2) for var in range(4)]
            x.append(jnp.concatenate([jnp.concatenate(parts[:4], axis=0), jnp.concatenate(parts[4:], axis=0)], axis=1))
        mean = [jnp.sum(a, axis=1, keepdims=True) * (1.0 / MEMBERS) for a in x]
        pert = [a - b for a, b in zip(x, mean)]
        patch = [patch_of(picked, c) for c in cs]
        w = [weight[pl.ds(c, 1), :] for c in cs]
        inv = [norms[pl.ds(c, 1), :] for c in cs]
        cross = []
        for i in todo:
            p = jnp.concatenate([patch[i][:, :MEMBERS], patch[i][:, MEMBERS:]], axis=0)
            cross.append(folded(dot_t(stacked(pert[i]), p), ROWS, PATCH) * (w[i] * inv[i] * (1.0 / (MEMBERS - 1.0))))
        force = [jnp.where(first_row, w[i] * gap[pl.ds(c, 1), :], 0.0) for i, c in enumerate(cs)]
        step = [patch_of(steps, c) for c in cs]
        once = [folded(dot(stacked(jnp.concatenate([cross[i], force[i]], axis=0)), step[i]), 48, PATCH) for i in todo]
        twice = [folded(dot(stacked(once[i][:ROWS]), step[i]), ROWS, PATCH) for i in todo]
        turn = [patch_of(turns, c) for c in cs]
        v, a, u, t1 = [], [], [], []
        for i in todo:
            t = inv[i]
            a0, a1 = 2.25 - 1.5 * t + 0.25 * t * t, 0.25 * t - 1.5
            v.append(jnp.concatenate([a0 * cross[i] + a1 * once[i][:ROWS] + 0.25 * twice[i], zeros], axis=0))
            t1.append(t * a0)
            a.append(1.5 - 0.5 * t)
            u.append(jnp.concatenate([-0.5 * cross[i], 1.5 * force[i] - 0.5 * once[i][ROWS:]], axis=0))

        def times_t1(a, u):
            new = [folded(dot(stacked(u[i]), turn[i]), 48, PATCH) + a[i] * v[i] for i in todo]
            return [a[i] * t1[i] for i in todo], new

        def times_f1(a, u):
            a2, u2 = times_t1(a, u)
            return [1.5 * a[i] - 0.5 * a2[i] for i in todo], [1.5 * u[i] - 0.5 * u2[i] for i in todo]
        a, u = times_f1(a, u)
        a2, u2 = times_f1(*times_f1(*times_t1(a, u)))
        a = [1.5 * a[i] - 0.5 * a2[i] for i in todo]
        u = [1.5 * u[i] - 0.5 * u2[i] for i in todo]
        spread = [folded(dot(stacked(u[i]), patch[i]), 48, MEMBERS) for i in todo]
        for i, c in enumerate(cs):
            scale = jnp.sqrt(inv[i])
            scale = jnp.concatenate([scale, scale], axis=1)
            share = jnp.concatenate([a[i], a[i]], axis=1)
            moved = (share * pert[i] + spread[i][:ROWS]) * scale
            nudge = spread[i][ROWS:ROWS + 1] * scale
            out = moved + (mean[i] + jnp.sum(moved * nudge, axis=1, keepdims=True) * (1.0 / (MEMBERS - 1.0)))
            for m in range(2):
                for var in range(4):
                    analysed[pl.ds((m * 4 + var) * 16 + c, 8, stride=128), :] = out[var * 8:var * 8 + 8, m * 128:m * 128 + 128]
        return carry
    lax.fori_loop(0, COLS // BATCH, body, 0)


def turn_members(src, dst):
    for level in range(LEVELS):
        dst[pl.ds(level * 128, 128), :] = jnp.transpose(src[pl.ds(level, MEM, stride=8), :])


def turn_back(src, dst):
    for level in range(LEVELS):
        dst[pl.ds(level, MEM, stride=8), :] = jnp.transpose(src[pl.ds(level * 128, 128), :])


def kernel(state, branch, site, value, index_all, weight, result,
           stab, stab_edge, to_next, to_prev, from_prev, from_next, mixed, edge, tiles, columns, obs, table,
           index, fields, lookup, turned, gap, analysed, picked, steps, turns, norms, outgoing, landed,
           halo_send, halo_recv, gather_sems, out_sems, in_sems, index_sem, arrived):
    me, tile = lax.axis_index("mem"), lax.axis_index("tile")
    greet(me, tile)
    rounds = pass_on(arrived, me, tile)
    next(rounds)
    fetch = pltpu.make_async_copy(index_all.at[0, pl.ds(pl.multiple_of(me * COLS, COLS), COLS)], index, index_sem)
    fetch.start()
    forecast_body(state, branch, stab, stab_edge, to_next, to_prev, from_prev, from_next, mixed, edge, halo_send, halo_recv, me, tile, rounds)
    slot = slot_of(me)
    here = pl.ds(pl.multiple_of(slot * 8, 8), 8)

    def send_columns():
        def body(i, carry):
            to = rem(me + i, MEM)
            send(tiles.at[pl.ds(pl.multiple_of(to * 8, 8), 8)], columns.at[here], out_sems.at[0], in_sems.at[0], to, tile)
            return carry
        lax.fori_loop(1, MEM, body, 0)
        columns[here, :] = tiles[pl.ds(pl.multiple_of(me * 8, 8), 8), :]

    observe(mixed, site, obs)
    table[pl.ds(pl.multiple_of(slot * 16, 16), 16), :] = obs[...]
    gather = gather_obs(table, gather_sems, me, tile)
    next(gather)
    cut_columns(mixed, tiles)
    for _ in rounds:
        pass
    next(gather)
    if ORDER == 0:
        send_columns()
        next(gather)
        next(gather)
    elif ORDER == 1:
        next(gather)
        send_columns()
        next(gather)
    else:
        next(gather)
        next(gather)
        send_columns()
    for _ in gather:
        pass
    fetch.wait()
    prepare(table, value, index, weight, lookup, turned, gap)
    pick_obs(turned, lookup, picked)
    sweep(turned, weight, picked, steps, turns, norms)
    wait_rows(tiles, out_sems.at[0], 8 * (MEM - 1))
    wait_rows(columns, in_sems.at[0], 8 * (MEM - 1))
    turn_members(columns, fields)
    apply(fields, weight, gap, picked, steps, turns, norms, analysed)
    turn_back(analysed, outgoing)
    mine = pl.ds(pl.multiple_of(me * 8, 8), 8)

    def give_back(i, carry):
        to = rem(me + i, MEM)
        send(outgoing.at[pl.ds(pl.multiple_of(slot_of(to) * 8, 8), 8)], landed.at[mine], out_sems.at[1], in_sems.at[1], to, tile)
        return carry
    lax.fori_loop(1, MEM, give_back, 0)
    landed[mine, :] = outgoing[here, :]
    wait_rows(outgoing, out_sems.at[1], 8 * (MEM - 1))
    wait_rows(landed, in_sems.at[1], 8 * (MEM - 1))
    place(landed, result)


ORDER = 0


def place(landed, result):
    def body(n, carry):
        x, lt = div(n, 4), rem(n, 4)
        blocks = [landed[pl.ds(pl.multiple_of((x * 32 + lt * 8 + g) * 8, 8), 8), :] for g in range(8)]
        blocks = block_transpose(blocks)
        for m in range(2):
            for var in range(4):
                result[pl.ds(lt * 256 + var * 64 + m * 4 + x, 8, stride=8), :] = blocks[m * 4 + var]
        return carry
    lax.fori_loop(0, 16, body, 0, unroll=4)


def shape(*dims, dtype=F32):
    return jax.ShapeDtypeStruct(dims, dtype)


def per_device(state, branch, obs_site, obs_value, patch_index, patch_weight):
    fields = state.reshape(ROWS, 8, WIDTH)
    dma = pltpu.SemaphoreType.DMA
    regular = pltpu.SemaphoreType.REGULAR

    def rows(n, width=LANES, dtype=F32):
        return pltpu.VMEM((n, width), dtype)
    result = pl.pallas_call(
        kernel,
        name="forecast_analysis",
        out_shape=shape(1024, LANES),
        in_specs=[VMEM, VMEM, VMEM, VMEM, ANY, VMEM],
        out_specs=VMEM,
        scratch_shapes=[
            rows(64), rows(64), rows(128, WIDTH), rows(128, WIDTH), rows(128, WIDTH), rows(128, WIDTH),
            rows(1024), rows(1024), rows(1024), rows(1024), rows(16), rows(MEM * 16),
            rows(COLS, LANES, jnp.int32), rows(1024), rows(OBS, 2 * MEMBERS, BF16), rows(LANES), rows(COLS), rows(1024),
            rows(COLS * PATCH, 2 * MEMBERS, BF16), rows(COLS * PATCH, 2 * PATCH, BF16), rows(COLS * PATCH, 2 * PATCH, BF16),
            rows(COLS), rows(1024), rows(1024),
            dma((2,)), dma((2,)), dma((8,)), dma((2,)), dma((2,)), dma(()), regular((4,)),
        ],
        compiler_params=pltpu.CompilerParams(collective_id=1, has_side_effects=True, vmem_limit_bytes=40 * 1024 * 1024),
    )(fields, branch, obs_site.reshape(8, LANES), obs_value.reshape(8, LANES), patch_index, patch_weight.reshape(COLS, LANES))
    return result.reshape(4, ROWS, 2, 4, LANES).transpose(1, 2, 3, 0, 4).reshape(state.shape)


def solution(mesh):
    placed = (
        P(None, None, "mem", "tile", None),
        P(),
        P("tile", None),
        P("tile", None),
        P("tile", None, None),
        P("tile", "mem", None),
    )
    return jax.shard_map(
        per_device,
        mesh=mesh,
        in_specs=placed,
        out_specs=P(None, None, "mem", "tile", None),
        check_vma=False,
    )
```

time: 133 us -> 92.2 us (0.69)
  Pallas kernels: 130 us -> 87 us
  local copies, waits for them, and re-layouts: 3.53 us -> 4.95 us
    pallas_call x3 -> x1, Pallas kernels: 130 us -> 87 us  [per_device(): pl.pallas_call(kernel, name='forecast_analysis', out_shape=shape(1024, LA...]
    unnamed x10, local copies, waits for them, and re-layouts: 0.77 us -> 2.21 us
where the time goes in v1:
time: 92.2 us; the launch traced here: 92 us
  Pallas kernels  87 us (94%)
  local copies, waits for them, and re-layouts  4.95 us (5%)
    pallas_call x1, Pallas kernels, per_device(): pl.pallas_call(kernel, name='forecast_analysis', out_shape=shape(1024, LA...  87 us
    unnamed x10, local copies, waits for them, and re-layouts  2.21 us

profile of v1, /device:TPU:1, one launch (start us, length us, event | category | flops | bytes accessed | tf_op | source)
XLA Modules:
  0.0 92.0 jit_solution(12807093632964551087)
XLA Ops:
  0.0 0.0 copy-start
  0.0 0.0 copy-start.3
  0.0 1.3 %reshape.18.state = f32[32,8,512]{2,1,0:T(8,128)S(1)} reshape(f32[4,8,2,4,512]{4,3,2,1,0:T(4,128)} %param.6) | data formatting | bytes 1048576 | tf_op jit(solution)/shard_map/reshape | solution.py:560
  1.3 0.1 copy-done
  1.4 0.0 copy-done.3
  1.4 0.0 copy-start.1
  1.4 0.8 copy-done.1
  2.1 0.0 copy-start.2
  2.1 0.7 copy-done.2
  2.8 0.0 copy-start.4
  2.8 0.7 copy-done.4
  3.5 87.0 %forecast_analysis.1 = f32[1024,128]{1,0:T(8,128)S(1)} custom-call(f32[32,8,512]{2,1,0:T(8,128)S(1)} %reshape.18.state, s32[16,512]{1,0:T(8,128)S(1)} %copy-done.1, s32[8,128]{1,0:T(8,128)S(1)} %bitcast.8, f32[8,128]{1,0:T(8,128)S(1)} %bitcast.9, s32[1,2048,128]{2,1,0:T(8,128)S(1)} %copy-done, f32[16,128]{1,0:T(8,128)S(1)} %bitcast.7), custom_call_target="tpu_custom_call" | custom-call | tf_op jit(solution)/shard_map/forecast_analysis/pallas_call | solution.py:566
  90.5 0.3 copy.7
  90.9 1.1 %reshape.23 = f32[4,8,2,4,512]{4,3,2,1,0:T(4,128)} reshape(f32[32,2,4,4,128]{4,3,2,1,0:T(4,128)S(1)} %copy.7) | data formatting | bytes 1048576 | tf_op jit(solution)/shard_map/reshape | solution.py:582
Async XLA Ops:
  0.0 1.4 %copy-start = (s32[1,2048,128]{2,1,0:T(8,128)S(1)}, s32[1,2048,128]{2,1,0:T(8,128)}, u32[]{:S(2)}) copy-start(s32[1,2048,128]{2,1,0:T(8,128)} %index_all.1) | copy-start | bytes 3145732
  0.0 1.4 %copy-start.3 = (s32[1,1024]{1,0:T(1,128)S(1)}, s32[1,1024]{1,0:T(1,128)}, u32[]{:S(2)}) copy-start(s32[1,1024]{1,0:T(1,128)} %param.8) | copy-start | bytes 12292
  1.4 0.8 copy-start.1
  2.1 0.7 copy-start.2
  2.8 0.7 copy-start.4

commit v2 on v1

--- a/solution.py
+++ b/solution.py
@@ -9,7 +9,7 @@
 F32 = jnp.float32
 BF16 = jnp.bfloat16
 VMEM = pl.BlockSpec(memory_space=pltpu.VMEM)
-ANY = pl.BlockSpec(memory_space=pl.ANY)
+HBM = pl.BlockSpec(memory_space=pltpu.HBM)
 LEVELS, ROWS, WIDTH, LANES = 8, 32, 512, 128
 MEM, COLS, MEMBERS, PATCH, OBS = 128, 16, 256, 128, 1024
 
@@ -150,19 +150,26 @@
         [src[pl.ds(pl.multiple_of(lt * 256 + row * 8, 8), 8), :] for lt in range(4)], axis=1)
 
 
-def forecast_body(state, branch, stab, stab_edge, to_next, to_prev, from_prev, from_next, mixed, edge, halo_send, halo_recv, me, tile, rounds):
+def forecast_body(state, branch, stab, stab_edge, to_next, to_prev, from_prev, from_next, mixed, edge, halo_send, halo_recv, me, tile, greeting, rounds, state_here, branch_here):
     sub = lax.broadcasted_iota(jnp.int32, (8, WIDTH), 0)
     next_tile, prev_tile = rem(tile + 1, 4), rem(tile + 3, 4)
+    state_here()
 
     def pack(row, carry):
         for q, (n_sub, p_sub) in enumerate(((3, 0), (7, 4), (2, 1), (6, 5))):
             to_next[pl.ds(row * 4 + q, 1), :] = state[row, pl.ds(n_sub, 1), :]
             to_prev[pl.ds(row * 4 + q, 1), :] = state[row, pl.ds(p_sub, 1), :]
         return carry
-    lax.fori_loop(0, ROWS, pack, 0)
-    send(to_next, from_prev, halo_send.at[0], halo_recv.at[0], me, next_tile)
-    send(to_prev, from_next, halo_send.at[1], halo_recv.at[1], me, prev_tile)
-
+    lax.fori_loop(0, ROWS, pack, 0, unroll=4)
+    for _ in greeting:
+        pass
+    for var in range(4):
+        rows = pl.ds(var * 32, 32)
+        send(to_next.at[rows], from_prev.at[rows], halo_send.at[0], halo_recv.at[var], me, next_tile)
+        send(to_prev.at[rows], from_next.at[rows], halo_send.at[1], halo_recv.at[4 + var], me, prev_tile)
+    next(rounds)
+
+    branch_here()
     own = [rows_of(branch, tile * 4 + x) for x in range(4)]
     before, after = rows_of(branch, rem(tile * 4 + 15, 16)), rows_of(branch, rem(tile * 4 + 4, 16))
     x_of = sub % 4
@@ -173,12 +180,6 @@
         for lt in range(4):
             ref[pl.ds(lt * 16, 8), :] = m[:, lt * LANES:(lt + 1) * LANES]
             ref[pl.ds(lt * 16 + 8, 8), :] = h[:, lt * LANES:(lt + 1) * LANES]
-
-    next(rounds)
-    wait_rows(to_next, halo_send.at[0], 128)
-    wait_rows(to_prev, halo_send.at[1], 128)
-    wait_rows(from_prev, halo_recv.at[0], 128)
-    wait_rows(from_next, halo_recv.at[1], 128)
     next(rounds)
 
     def pick(a, b, c, d):
@@ -196,7 +197,10 @@
         outer = pick(left[2], left[3], right[2], right[3])
         put_tiles(edge, row, laplace_step(edge_centre, outer, pick(*inner)))
         return carry
-    lax.fori_loop(0, ROWS, first, 0, unroll=4)
+    for var in range(4):
+        wait_rows(from_prev, halo_recv.at[var], 32)
+        wait_rows(from_next, halo_recv.at[4 + var], 32)
+        lax.fori_loop(var * 8, var * 8 + 8, first, 0, unroll=4)
     mix_columns(mixed, mixed, stab)
     mix_columns(edge, edge, stab_edge)
     next(rounds)
@@ -211,6 +215,8 @@
         return carry
     lax.fori_loop(0, ROWS, second, 0, unroll=4)
     mix_columns(mixed, mixed, stab)
+    wait_rows(to_next, halo_send.at[0], 128)
+    wait_rows(to_prev, halo_send.at[1], 128)
 
 
 def observe(mixed, site, obs):
@@ -251,24 +257,72 @@
     lax.fori_loop(0, 16, body, 0, unroll=4)
 
 
-def gather_obs(table, sems, me, tile):
-    core, y, x = rem(me, 2), rem(div(me, 2), 8), div(me, 32)
-    starts = (slot_of(me), core * 64 + x * 16 + y * 2, core * 64 + x * 16, core * 64)
-    for n, (group, start, count) in enumerate(zip(near(me), starts, (1, 2, 16, 64))):
-        rows = count * 16
-        block = table.at[pl.ds(pl.multiple_of(start * 16, rows), rows)]
-        for to in group:
-            send(block, block, sems.at[2 * n], sems.at[2 * n + 1], to, tile)
-        yield
-        wait_rows(table, sems.at[2 * n], rows * len(group))
-        wait_rows(table, sems.at[2 * n + 1], rows * len(group))
+def gather_obs(table, send_sems, plane_sems, x_sems, core_sem, me, tile):
+    core, y, z, x = rem(me, 2), rem(div(me, 2), 8), rem(div(me, 16), 2), div(me, 32)
+
+    def part(first, count):
+        return table.at[pl.ds(pl.multiple_of(first * 16, count * 16), count * 16)]
+
+    def slot(y_of, z_of):
+        return part(core * 64 + x * 16 + y_of * 2 + z_of, 1)
+
+    def pass_slot(one):
+        for j in (2, 1, 3):
+            send(one, one, send_sems.at[1], x_sems.at[j - 1], device_at(core, rem(x + j, 4), y, z), tile)
+        send(one, one, send_sems.at[2], core_sem, device_at(1 - core, x, y, z), tile)
+    own = slot(y, z)
+    for i in (4, 3, 5, 2, 6, 1, 7, 0):
+        send(own, own, send_sems.at[0], plane_sems.at[7 + i], device_at(core, x, rem(y + i, 8), 1 - z), tile)
+        if i:
+            send(own, own, send_sems.at[0], plane_sems.at[i - 1], device_at(core, x, rem(y + i, 8), z), tile)
+    pass_slot(own)
+    yield
+    for i in (1, 7, 2, 6, 3, 5, 4):
+        wait_rows(table, plane_sems.at[i - 1], 16)
+        pass_slot(slot(rem(y + 8 - i, 8), z))
+    for i in (0, 1, 7, 2, 6, 3, 5, 4):
+        wait_rows(table, plane_sems.at[7 + i], 16)
+        pass_slot(slot(rem(y + 8 - i, 8), 1 - z))
+    yield
+    for j in (1, 3, 2):
+        wait_rows(table, x_sems.at[j - 1], 256)
+        plane = part(core * 64 + rem(x + 4 - j, 4) * 16, 16)
+        send(plane, plane, send_sems.at[2], core_sem, device_at(1 - core, x, y, z), tile)
+    wait_rows(table, core_sem, 1024)
+    wait_rows(table, send_sems.at[0], 16 * 15)
+    wait_rows(table, send_sems.at[1], 256 * 3)
+    wait_rows(table, send_sems.at[2], 1024)
+
+
+def each_device(me, do):
+    core, y, z, x = rem(me, 2), rem(div(me, 2), 8), rem(div(me, 16), 2), div(me, 32)
+
+    def all_at(y_to, z_to, own):
+        for i in (2, 1, 3, 0):
+            for c in (1, 0):
+                if not (own and i == 0 and c == 0):
+                    do(device_at(rem(core + c, 2), rem(x + i, 4), y_to, z_to))
+
+    def far(n, carry):
+        half = div(n + 1, 2)
+        step = rem(12 + (2 * rem(n, 2) - 1) * half, 8)
+        all_at(rem(y + step, 8), 1 - z, False)
+        return carry
+
+    def close(n, carry):
+        half = div(n + 1, 2)
+        step = rem(12 + (2 * rem(n, 2) - 1) * half, 8)
+        all_at(rem(y + step, 8), z, False)
+        return carry
+    lax.fori_loop(0, 8, far, 0)
+    lax.fori_loop(0, 7, close, 0)
+    all_at(y, z, True)
 
 
 def near(me):
     core, y, z, x = rem(me, 2), rem(div(me, 2), 8), rem(div(me, 16), 2), div(me, 32)
     return (
-        [device_at(core, x, y, 1 - z)],
-        [device_at(core, x, rem(y + i, 8), z) for i in range(1, 8)],
+        [device_at(core, x, rem(y + i, 8), z) for i in range(1, 8)] + [device_at(core, x, rem(y + i, 8), 1 - z) for i in range(8)],
         [device_at(core, rem(x + i, 4), y, z) for i in range(1, 4)],
         [device_at(1 - core, x, y, z)],
     )
@@ -281,7 +335,8 @@
     for group in near(me):
         for to in group:
             pl.semaphore_signal(barrier, inc=1, device_id=(to, tile), device_id_type=MESH)
-    pl.semaphore_wait(barrier, 14)
+    yield
+    pl.semaphore_wait(barrier, 2 + 15 + 3 + 1)
 
 
 def pass_on(arrived, me, tile):
@@ -471,51 +526,52 @@
         dst[pl.ds(level, MEM, stride=8), :] = jnp.transpose(src[pl.ds(level * 128, 128), :])
 
 
-def kernel(state, branch, site, value, index_all, weight, result,
-           stab, stab_edge, to_next, to_prev, from_prev, from_next, mixed, edge, tiles, columns, obs, table,
-           index, fields, lookup, turned, gap, analysed, picked, steps, turns, norms, outgoing, landed,
-           halo_send, halo_recv, gather_sems, out_sems, in_sems, index_sem, arrived):
+def kernel(state_in, branch_in, site_in, value_in, index_in, weight_in, result,
+           state, branch, site, value, weight, stab, stab_edge, to_next, to_prev, from_prev, from_next, mixed, edge, tiles, columns, obs, table,
+           index, fields, lookup, turned, gap, analysed, picked, steps, turns, norms, outgoing, landed, placed,
+           halo_send, halo_recv, send_sems, plane_sems, x_sems, core_sem, out_sems, in_sems, load_sems, store_sems, arrived):
     me, tile = lax.axis_index("mem"), lax.axis_index("tile")
-    greet(me, tile)
+    greeting = greet(me, tile)
+    next(greeting)
+    loads = [pltpu.make_async_copy(state_in.at[:, m], state.at[:, pl.ds(m * 4, 4)], load_sems.at[m]) for m in range(2)]
+    loads += [pltpu.make_async_copy(a, b, load_sems.at[2 + n]) for n, (a, b) in enumerate(
+        ((branch_in, branch), (site_in, site), (value_in, value), (weight_in, weight),
+         (index_in.at[0, pl.ds(pl.multiple_of(me * COLS, COLS), COLS)], index)))]
+    for load in loads:
+        load.start()
+
+    def state_here():
+        loads[0].wait()
+        loads[1].wait()
     rounds = pass_on(arrived, me, tile)
-    next(rounds)
-    fetch = pltpu.make_async_copy(index_all.at[0, pl.ds(pl.multiple_of(me * COLS, COLS), COLS)], index, index_sem)
-    fetch.start()
-    forecast_body(state, branch, stab, stab_edge, to_next, to_prev, from_prev, from_next, mixed, edge, halo_send, halo_recv, me, tile, rounds)
+    forecast_body(state, branch, stab, stab_edge, to_next, to_prev, from_prev, from_next, mixed, edge, halo_send, halo_recv, me, tile,
+                  greeting, rounds, state_here, loads[2].wait)
+    for load in loads[3:]:
+        load.wait()
     slot = slot_of(me)
     here = pl.ds(pl.multiple_of(slot * 8, 8), 8)
 
     def send_columns():
-        def body(i, carry):
-            to = rem(me + i, MEM)
+        def to_owner(to):
             send(tiles.at[pl.ds(pl.multiple_of(to * 8, 8), 8)], columns.at[here], out_sems.at[0], in_sems.at[0], to, tile)
-            return carry
-        lax.fori_loop(1, MEM, body, 0)
+        each_device(me, to_owner)
         columns[here, :] = tiles[pl.ds(pl.multiple_of(me * 8, 8), 8), :]
 
     observe(mixed, site, obs)
     table[pl.ds(pl.multiple_of(slot * 16, 16), 16), :] = obs[...]
-    gather = gather_obs(table, gather_sems, me, tile)
+    gather = gather_obs(table, send_sems, plane_sems, x_sems, core_sem, me, tile)
     next(gather)
     cut_columns(mixed, tiles)
     for _ in rounds:
         pass
-    next(gather)
     if ORDER == 0:
-        send_columns()
-        next(gather)
-        next(gather)
-    elif ORDER == 1:
-        next(gather)
         send_columns()
         next(gather)
     else:
         next(gather)
-        next(gather)
         send_columns()
     for _ in gather:
         pass
-    fetch.wait()
     prepare(table, value, index, weight, lookup, turned, gap)
     pick_obs(turned, lookup, picked)
     sweep(turned, weight, picked, steps, turns, norms)
@@ -526,18 +582,23 @@
     turn_back(analysed, outgoing)
     mine = pl.ds(pl.multiple_of(me * 8, 8), 8)
 
-    def give_back(i, carry):
-        to = rem(me + i, MEM)
+    def give_back(to):
         send(outgoing.at[pl.ds(pl.multiple_of(slot_of(to) * 8, 8), 8)], landed.at[mine], out_sems.at[1], in_sems.at[1], to, tile)
-        return carry
-    lax.fori_loop(1, MEM, give_back, 0)
+    each_device(me, give_back)
     landed[mine, :] = outgoing[here, :]
     wait_rows(outgoing, out_sems.at[1], 8 * (MEM - 1))
     wait_rows(landed, in_sems.at[1], 8 * (MEM - 1))
-    place(landed, result)
-
-
-ORDER = 0
+    place(landed, placed)
+    whole = placed.reshape(4, ROWS, 8, LANES)
+    stores = [pltpu.make_async_copy(whole.at[lt, :, pl.ds(m * 4, 4)], result.at[:, m, :, pl.ds(lt * LANES, LANES)], store_sems.at[lt * 2 + m])
+              for lt in range(4) for m in range(2)]
+    for store in stores:
+        store.start()
+    for store in stores:
+        store.wait()
+
+
+ORDER = 1
 
 
 def place(landed, result):
@@ -557,7 +618,6 @@
 
 
 def per_device(state, branch, obs_site, obs_value, patch_index, patch_weight):
-    fields = state.reshape(ROWS, 8, WIDTH)
     dma = pltpu.SemaphoreType.DMA
     regular = pltpu.SemaphoreType.REGULAR
 
@@ -566,20 +626,21 @@
     result = pl.pallas_call(
         kernel,
         name="forecast_analysis",
-        out_shape=shape(1024, LANES),
-        in_specs=[VMEM, VMEM, VMEM, VMEM, ANY, VMEM],
-        out_specs=VMEM,
+        out_shape=shape(ROWS, 2, 4, WIDTH),
+        in_specs=[HBM] * 6,
+        out_specs=HBM,
         scratch_shapes=[
+            pltpu.VMEM((ROWS, 8, WIDTH), F32), pltpu.VMEM((16, WIDTH), jnp.int32), rows(8, dtype=jnp.int32), rows(8), rows(COLS),
             rows(64), rows(64), rows(128, WIDTH), rows(128, WIDTH), rows(128, WIDTH), rows(128, WIDTH),
             rows(1024), rows(1024), rows(1024), rows(1024), rows(16), rows(MEM * 16),
             rows(COLS, LANES, jnp.int32), rows(1024), rows(OBS, 2 * MEMBERS, BF16), rows(LANES), rows(COLS), rows(1024),
             rows(COLS * PATCH, 2 * MEMBERS, BF16), rows(COLS * PATCH, 2 * PATCH, BF16), rows(COLS * PATCH, 2 * PATCH, BF16),
-            rows(COLS), rows(1024), rows(1024),
-            dma((2,)), dma((2,)), dma((8,)), dma((2,)), dma((2,)), dma(()), regular((4,)),
+            rows(COLS), rows(1024), rows(1024), rows(1024),
+            dma((2,)), dma((8,)), dma((3,)), dma((15,)), dma((3,)), dma(()), dma((2,)), dma((2,)), dma((7,)), dma((8,)), regular((3,)),
         ],
-        compiler_params=pltpu.CompilerParams(collective_id=1, has_side_effects=True, vmem_limit_bytes=40 * 1024 * 1024),
-    )(fields, branch, obs_site.reshape(8, LANES), obs_value.reshape(8, LANES), patch_index, patch_weight.reshape(COLS, LANES))
-    return result.reshape(4, ROWS, 2, 4, LANES).transpose(1, 2, 3, 0, 4).reshape(state.shape)
+        compiler_params=pltpu.CompilerParams(collective_id=1, has_side_effects=True, vmem_limit_bytes=60 * 1024 * 1024),
+    )(state.reshape(ROWS, 2, 4, WIDTH), branch, obs_site.reshape(8, LANES), obs_value.reshape(8, LANES), patch_index, patch_weight.reshape(COLS, LANES))
+    return result.reshape(state.shape)
 
 
 def solution(mesh):

time: 92.2 us -> 84.7 us (0.919)
  Pallas kernels: 87 us -> 82.7 us
  local copies, waits for them, and re-layouts: 4.95 us -> 1.87 us
    pallas_call x1, Pallas kernels: 87 us -> 82.7 us  [per_device(): pl.pallas_call(kernel, name='forecast_analysis', out_shape=shape(ROWS, 2,...]
    reshape x2 -> x0, local copies, waits for them, and re-layouts: 2.4 us -> none  [the longest x1 1.31 us: per_device(): fields = state.reshape(ROWS, 8, WIDTH)]
    unnamed x10 -> x1, local copies, waits for them, and re-layouts: 2.21 us -> 1.87 us
where the time goes in v2:
time: 84.7 us; the launch traced here: 84.5 us
  Pallas kernels  82.7 us (98%)
  local copies, waits for them, and re-layouts  1.87 us (2%)
    pallas_call x1, Pallas kernels, per_device(): pl.pallas_call(kernel, name='forecast_analysis', out_shape=shape(ROWS, 2,...  82.7 us
    unnamed x1, local copies, waits for them, and re-layouts  1.87 us

profile of v2, /device:TPU:1, one launch (start us, length us, event | category | flops | bytes accessed | tf_op | source)
XLA Modules:
  0.0 84.5 jit_solution(13984693711813392718)
XLA Ops:
  0.0 82.7 %forecast_analysis.1 = f32[32,2,4,512]{3,2,1,0:T(4,128)} custom-call(f32[32,2,4,512]{3,2,1,0:T(4,128)} %bitcast.6, s32[16,512]{1,0:T(8,128)} %branch_in.1, s32[8,128]{1,0:T(8,128)} %bitcast.8, f32[8,128]{1,0:T(8,128)} %bitcast.9, s32[1,2048,128]{2,1,0:T(8,128)} %index_in.1, f32[16,128]{1,0:T(8,128)} %bitcast.7), custom_call_target="tpu_custom_call" | custom-call | tf_op jit(solution)/shard_map/forecast_analysis/pallas_call | solution.py:626
  82.7 1.9 %copy.8 = f32[4,8,2,4,512]{4,3,2,1,0:T(4,128)} copy(f32[4,8,2,4,512]{4,3,2,1,0:T(4,128)} %bitcast.5) | data formatting | bytes 1048576

commit v3 on v2

--- a/solution.py
+++ b/solution.py
@@ -150,7 +150,7 @@
         [src[pl.ds(pl.multiple_of(lt * 256 + row * 8, 8), 8), :] for lt in range(4)], axis=1)
 
 
-def forecast_body(state, branch, stab, stab_edge, to_next, to_prev, from_prev, from_next, mixed, edge, halo_send, halo_recv, me, tile, greeting, rounds, state_here, branch_here):
+def forecast_body(state, branch, stab, stab_edge, to_next, to_prev, from_prev, from_next, mixed, edge, halo_send, halo_recv, me, tile, greeting, rounds, state_here, branch_here, meanwhile):
     sub = lax.broadcasted_iota(jnp.int32, (8, WIDTH), 0)
     next_tile, prev_tile = rem(tile + 1, 4), rem(tile + 3, 4)
     state_here()
@@ -181,6 +181,7 @@
             ref[pl.ds(lt * 16, 8), :] = m[:, lt * LANES:(lt + 1) * LANES]
             ref[pl.ds(lt * 16 + 8, 8), :] = h[:, lt * LANES:(lt + 1) * LANES]
     next(rounds)
+    meanwhile()
 
     def pick(a, b, c, d):
         return jnp.where(x_of == 0, a, jnp.where(x_of == 1, b, jnp.where(x_of == 2, c, d)))
@@ -200,7 +201,7 @@
     for var in range(4):
         wait_rows(from_prev, halo_recv.at[var], 32)
         wait_rows(from_next, halo_recv.at[4 + var], 32)
-        lax.fori_loop(var * 8, var * 8 + 8, first, 0, unroll=4)
+        lax.fori_loop(var * 8, var * 8 + 8, first, 0, unroll=8)
     mix_columns(mixed, mixed, stab)
     mix_columns(edge, edge, stab_edge)
     next(rounds)
@@ -213,38 +214,56 @@
         down = jnp.where(x_of == 3, jnp.where(sub < 4, side[2], side[3]), pltpu.roll(centre, 7, 0))
         put_tiles(mixed, row, laplace_step(centre, up, down))
         return carry
-    lax.fori_loop(0, ROWS, second, 0, unroll=4)
+    lax.fori_loop(0, ROWS, second, 0, unroll=8)
     mix_columns(mixed, mixed, stab)
     wait_rows(to_next, halo_send.at[0], 128)
     wait_rows(to_prev, halo_send.at[1], 128)
 
 
-def observe(mixed, site, obs):
-    sub = lax.broadcasted_iota(jnp.int32, (8, LANES), 0)
-    sites = site[...]
-    lane, x = sites % 128, (sites // 512) % 4
-    key = (sites // 2048) * 4 + (sites // 128) % 4
-
-    def spread(a, b):
-        return jnp.broadcast_to(a[b:b + 1, :], (8, LANES))
-    lanes = [spread(lane, b) for b in range(8)]
-    keys = [spread(key, b) for b in range(8)]
-
-    accs = []
-    for b in range(8):
-        def body(row, acc):
-            for lt in range(4):
-                tile = mixed[pl.ds(pl.multiple_of(lt * 256 + row * 8, 8), 8), :]
-                found = jnp.take_along_axis(tile, lanes[b], axis=1, mode="promise_in_bounds")
-                acc = jnp.where(keys[b] == row * 4 + lt, found, acc)
-            return acc
-        accs.append(lax.fori_loop(0, ROWS, body, jnp.zeros((8, LANES), F32), unroll=8))
-    for b in range(8):
-        only = jnp.where(sub % 4 == spread(x, b), accs[b], 0.0)
-        only = only + pltpu.roll(only, 7, 0)
-        only = only + pltpu.roll(only, 6, 0)
-        obs[pl.ds(b, 1), :] = only[0:1, :]
-        obs[pl.ds(8 + b, 1), :] = only[4:5, :]
+def mark_sites(site, sites_at):
+    columns = site[...] % 2048
+
+    def body(n, carry):
+        rows = pl.ds(pl.multiple_of(n * 256, 256), 256)
+        place = lax.broadcasted_iota(jnp.int32, (256, LANES), 0) + n * 256
+        for b in range(8):
+            sites_at[rows, pl.ds(b * LANES, LANES)] = (place == columns[b:b + 1, :]).astype(F32).astype(BF16)
+        return carry
+    lax.fori_loop(0, 8, body, 0)
+
+
+def mark_patch(index, weight, turned, chosen):
+    turned[...] = jnp.transpose(jnp.concatenate([index[...].astype(F32), weight[...], jnp.zeros((96, LANES), F32)], axis=0))
+    places = lax.broadcasted_iota(jnp.int32, (PATCH, OBS), 1)
+
+    def body(n, carry):
+        here = pltpu.roll(turned[...], LANES - n * 2, 1)
+        for i in range(2):
+            rows = pl.ds(pl.multiple_of((n * 2 + i) * PATCH, PATCH), PATCH)
+            chosen[rows, :] = (places == here[:, i:i + 1].astype(jnp.int32)).astype(F32).astype(BF16)
+        return carry
+    lax.fori_loop(0, COLS // 2, body, 0)
+
+
+def observe(mixed, site, sites_at, parts, obs):
+    def body(n, carry):
+        x, lt = div(n, 4), rem(n, 4)
+        left = jnp.concatenate([mixed[pl.ds(lt * 256 + var * 64 + m * 4 + x, 8, stride=8), :] for m in range(2) for var in range(4)], axis=0)
+        for part in range(3):
+            piece = left.astype(BF16)
+            parts[pl.ds(part * 64, 64), pl.ds(pl.multiple_of(n * LANES, LANES), LANES)] = piece
+            left = left - piece.astype(F32)
+        return carry
+    lax.fori_loop(0, 16, body, 0, unroll=4)
+    row = lax.broadcasted_iota(jnp.int32, (ROWS, LANES), 0)
+    wanted = site[...] // 2048
+    for b in range(0, 8, 2):
+        found = dot(parts[...], sites_at[:, b * LANES:(b + 2) * LANES])
+        found = found[:64] + (found[64:128] + found[128:])
+        for i in range(2):
+            for m in range(2):
+                one = jnp.where(row == wanted[b + i:b + i + 1, :], found[m * ROWS:(m + 1) * ROWS, i * LANES:(i + 1) * LANES], 0.0)
+                obs[pl.ds(m * 8 + b + i, 1), :] = jnp.sum(one, axis=0, keepdims=True)
 
 
 def cut_columns(mixed, tiles):
@@ -303,19 +322,15 @@
                 if not (own and i == 0 and c == 0):
                     do(device_at(rem(core + c, 2), rem(x + i, 4), y_to, z_to))
 
-    def far(n, carry):
-        half = div(n + 1, 2)
-        step = rem(12 + (2 * rem(n, 2) - 1) * half, 8)
-        all_at(rem(y + step, 8), 1 - z, False)
-        return carry
-
-    def close(n, carry):
-        half = div(n + 1, 2)
-        step = rem(12 + (2 * rem(n, 2) - 1) * half, 8)
-        all_at(rem(y + step, 8), z, False)
-        return carry
-    lax.fori_loop(0, 8, far, 0)
-    lax.fori_loop(0, 7, close, 0)
+    def body(z_to):
+        def one(n, carry):
+            half = div(n + 1, 2)
+            step = rem(12 + (2 * rem(n, 2) - 1) * half, 8)
+            all_at(rem(y + step, 8), z_to, False)
+            return carry
+        return one
+    lax.fori_loop(0, 8, body(1 - z), 0)
+    lax.fori_loop(0, 7, body(z), 0)
     all_at(y, z, True)
 
 
@@ -365,7 +380,7 @@
     return dot(high, pair[0]) + (dot(low, pair[0]) + dot(high, pair[1]))
 
 
-def prepare(table, value, index, weight, lookup, turned, gap):
+def prepare(table, value, index, lookup, gap):
     total = table[pl.ds(0, 16), :]
     total = lax.fori_loop(1, MEM, lambda s, t: t + table[pl.ds(pl.multiple_of(s * 16, 16), 16), :], total)
     mean = (total[:8] + total[8:]) * (1.0 / MEMBERS)
@@ -377,8 +392,6 @@
             lookup[pl.ds(b * 128, 128), pl.ds(m * 128, 128)] = high
             lookup[pl.ds(b * 128, 128), pl.ds(256 + m * 128, 128)] = low
     indices = index[...]
-    both = jnp.concatenate([indices.astype(F32), weight[...], jnp.zeros((96, LANES), F32)], axis=0)
-    turned[...] = jnp.transpose(both)
     for part in range(2):
         own = indices[part * 8:part * 8 + 8]
         found = jnp.zeros((8, LANES), F32)
@@ -406,114 +419,89 @@
     return (p[:rows, :width] + p[rows:, :width]) + (p[:rows, width:] + p[rows:, width:])
 
 
-GROUP = 4
-BATCH = 4
-
-
-def pick_obs(turned, lookup, picked):
-    places = lax.broadcasted_iota(jnp.int32, (PATCH, OBS), 1)
-
-    def body(n, carry):
-        here = pltpu.roll(turned[...], LANES - n * GROUP, 1)
-        chosen = [(places == here[:, i:i + 1].astype(jnp.int32)).astype(F32).astype(BF16) for i in range(GROUP)]
-        rows = GROUP * PATCH
-        found = dot(jnp.concatenate(chosen, axis=0), lookup[...])
-        picked[pl.ds(pl.multiple_of(n * rows, rows), rows), :] = found.astype(BF16)
-        return carry
-    lax.fori_loop(0, COLS // GROUP, body, 0)
+def pick_obs(chosen, lookup, picked):
+    for n in range(2):
+        rows = pl.ds(n * 1024, 1024)
+        picked[rows, :] = dot(chosen[rows, :], lookup[...]).astype(BF16)
 
 
 def patch_of(picked, c):
     return picked[pl.ds(pl.multiple_of(c * PATCH, PATCH), PATCH), :]
 
 
-def sweep(turned, weight, picked, steps, turns, norms):
-    def body(n, carry):
-        one = eye()
-        here = pltpu.roll(turned[...], LANES - n * BATCH, 1)
-        cs = [n * BATCH + i for i in range(BATCH)]
-        both = [patch_of(picked, c) for c in cs]
-        both = [jnp.concatenate([p[:, :MEMBERS], p[:, MEMBERS:]], axis=0) for p in both]
-        cov = [folded(dot_t(q, q), PATCH, PATCH) for q in both]
-        cov_w = [v * (weight[pl.ds(c, 1), :] * (1.0 / (MEMBERS - 1.0))) for v, c in zip(cov, cs)]
-        inv = []
-        for i in range(BATCH):
-            column = here[:, COLS + i:COLS + i + 1] * (1.0 / (MEMBERS - 1.0))
-            total = jnp.sum(cov_w[i] * (2.0 * one + cov[i] * column), axis=0, keepdims=True)
-            total = jnp.sum(total, axis=1, keepdims=True)
-            inv.append(jnp.broadcast_to(1.0 / jnp.sqrt(MEMBERS + total), (1, PATCH)))
-        step = [(one + v) * t for v, t in zip(cov_w, inv)]
-        parts = [split(k) for k in step]
-        wide = [jnp.concatenate(p, axis=1) for p in parts]
-        square = [folded(dot(jnp.concatenate(p, axis=0), k), PATCH, PATCH) for p, k in zip(parts, wide)]
-        inner = [2.25 * one - 1.5 * k + 0.25 * q for k, q in zip(step, square)]
-        turn = [folded(dot(stacked(g), k), PATCH, PATCH) for g, k in zip(inner, wide)]
-        for i, c in enumerate(cs):
-            here_rows = pl.ds(pl.multiple_of(c * PATCH, PATCH), PATCH)
-            steps[here_rows, :] = wide[i]
-            turns[here_rows, :] = beside(turn[i])
-            norms[pl.ds(c, 1), :] = inv[i]
-        return carry
-    lax.fori_loop(0, COLS // BATCH, body, 0)
-
-
-def apply(fields, weight, gap, picked, steps, turns, norms, analysed):
-    def body(n, carry):
-        cs = [n * BATCH + i for i in range(BATCH)]
-        todo = range(BATCH)
-        first_row = lax.broadcasted_iota(jnp.int32, (16, PATCH), 0) == 0
-        zeros = jnp.zeros((16, PATCH), F32)
-        x = []
-        for c in cs:
-            parts = [fields[pl.ds((m * 4 + var) * 16 + c, 8, stride=128), :] for m in range(2) for var in range(4)]
-            x.append(jnp.concatenate([jnp.concatenate(parts[:4], axis=0), jnp.concatenate(parts[4:], axis=0)], axis=1))
-        mean = [jnp.sum(a, axis=1, keepdims=True) * (1.0 / MEMBERS) for a in x]
-        pert = [a - b for a, b in zip(x, mean)]
-        patch = [patch_of(picked, c) for c in cs]
-        w = [weight[pl.ds(c, 1), :] for c in cs]
-        inv = [norms[pl.ds(c, 1), :] for c in cs]
-        cross = []
-        for i in todo:
-            p = jnp.concatenate([patch[i][:, :MEMBERS], patch[i][:, MEMBERS:]], axis=0)
-            cross.append(folded(dot_t(stacked(pert[i]), p), ROWS, PATCH) * (w[i] * inv[i] * (1.0 / (MEMBERS - 1.0))))
-        force = [jnp.where(first_row, w[i] * gap[pl.ds(c, 1), :], 0.0) for i, c in enumerate(cs)]
-        step = [patch_of(steps, c) for c in cs]
-        once = [folded(dot(stacked(jnp.concatenate([cross[i], force[i]], axis=0)), step[i]), 48, PATCH) for i in todo]
-        twice = [folded(dot(stacked(once[i][:ROWS]), step[i]), ROWS, PATCH) for i in todo]
-        turn = [patch_of(turns, c) for c in cs]
-        v, a, u, t1 = [], [], [], []
-        for i in todo:
-            t = inv[i]
-            a0, a1 = 2.25 - 1.5 * t + 0.25 * t * t, 0.25 * t - 1.5
-            v.append(jnp.concatenate([a0 * cross[i] + a1 * once[i][:ROWS] + 0.25 * twice[i], zeros], axis=0))
-            t1.append(t * a0)
-            a.append(1.5 - 0.5 * t)
-            u.append(jnp.concatenate([-0.5 * cross[i], 1.5 * force[i] - 0.5 * once[i][ROWS:]], axis=0))
-
-        def times_t1(a, u):
-            new = [folded(dot(stacked(u[i]), turn[i]), 48, PATCH) + a[i] * v[i] for i in todo]
-            return [a[i] * t1[i] for i in todo], new
-
-        def times_f1(a, u):
-            a2, u2 = times_t1(a, u)
-            return [1.5 * a[i] - 0.5 * a2[i] for i in todo], [1.5 * u[i] - 0.5 * u2[i] for i in todo]
-        a, u = times_f1(a, u)
-        a2, u2 = times_f1(*times_f1(*times_t1(a, u)))
-        a = [1.5 * a[i] - 0.5 * a2[i] for i in todo]
-        u = [1.5 * u[i] - 0.5 * u2[i] for i in todo]
-        spread = [folded(dot(stacked(u[i]), patch[i]), 48, MEMBERS) for i in todo]
-        for i, c in enumerate(cs):
-            scale = jnp.sqrt(inv[i])
-            scale = jnp.concatenate([scale, scale], axis=1)
-            share = jnp.concatenate([a[i], a[i]], axis=1)
-            moved = (share * pert[i] + spread[i][:ROWS]) * scale
-            nudge = spread[i][ROWS:ROWS + 1] * scale
-            out = moved + (mean[i] + jnp.sum(moved * nudge, axis=1, keepdims=True) * (1.0 / (MEMBERS - 1.0)))
-            for m in range(2):
-                for var in range(4):
-                    analysed[pl.ds((m * 4 + var) * 16 + c, 8, stride=128), :] = out[var * 8:var * 8 + 8, m * 128:m * 128 + 128]
-        return carry
-    lax.fori_loop(0, COLS // BATCH, body, 0)
+def sweep(turned, weight, gap, picked, turns, norms, shares, nudges):
+    columns = range(COLS)
+    one = eye()
+
+    def c_rate(t):
+        return 2.25 - 1.5 * t + 0.25 * t * t
+
+    def h(t, y, square):
+        return c_rate(t) * one + (0.25 * t - 1.5) * y + 0.25 * square
+
+    def times(a, wide):
+        return [folded(dot(stacked(m), k), m.shape[0], PATCH) for m, k in zip(a, wide)]
+    patch = [patch_of(picked, c) for c in columns]
+    both = [jnp.concatenate([p[:, :MEMBERS], p[:, MEMBERS:]], axis=0) for p in patch]
+    cov = [folded(dot_t(q, q), PATCH, PATCH) for q in both]
+    cov_w = [v * (weight[pl.ds(c, 1), :] * (1.0 / (MEMBERS - 1.0))) for v, c in zip(cov, columns)]
+    t = []
+    for c in columns:
+        column = turned[:, COLS + c:COLS + c + 1] * (1.0 / (MEMBERS - 1.0))
+        total = jnp.sum(cov_w[c] * (2.0 * one + cov[c] * column), axis=0, keepdims=True)
+        total = jnp.sum(total, axis=1, keepdims=True)
+        t.append(jnp.broadcast_to(1.0 / jnp.sqrt(MEMBERS + total), (1, PATCH)))
+    k = [(one + v) * r for v, r in zip(cov_w, t)]
+    k_wide = [beside(m) for m in k]
+    k_square = times(k, k_wide)
+    h_k = [h(r, m, q) for r, m, q in zip(t, k, k_square)]
+    turn = times([2.25 * one - 1.5 * m + 0.25 * q for m, q in zip(k, k_square)], k_wide)
+    t1 = [r * c_rate(r) for r in t]
+    turn_wide = [beside(m) for m in turn]
+    turn_square = times(turn, turn_wide)
+    second = times([2.25 * one - 1.5 * m + 0.25 * q for m, q in zip(turn, turn_square)], turn_wide)
+    f0, f1 = [1.5 - 0.5 * r for r in t], [1.5 - 0.5 * r for r in t1]
+    f2 = [1.5 - 0.5 * r * c_rate(r) for r in t1]
+    left = times([1.5 * one - 0.5 * m + a * b for m, a, b in zip(turn, f0, h_k)], [beside(1.5 * one - 0.5 * m) for m in second])
+    right = times([a * b * m for a, b, m in zip(f0, f1, h_k)], [beside(h(r, m, q)) for r, m, q in zip(t1, turn, turn_square)])
+    wide = [beside(-0.5 * (a + b)) for a, b in zip(left, right)]
+    first_row = lax.broadcasted_iota(jnp.int32, (16, PATCH), 0) == 0
+    force = [jnp.where(first_row, weight[pl.ds(c, 1), :] * gap[pl.ds(c, 1), :], 0.0) for c in columns]
+    share = [a * b * c for a, b, c in zip(f0, f1, f2)]
+    ahead = [m - r * a for m, r, a in zip(times(force, k_wide), t, force)]
+    force = [a * b + m for a, b, m in zip(share, force, times(ahead, wide))]
+    for c in columns:
+        turns[pl.ds(c * PATCH, PATCH), :] = wide[c]
+        norms[pl.ds(c, 1), :] = t[c]
+        shares[pl.ds(c, 1), :] = share[c]
+        scale = jnp.sqrt(t[c])
+        nudges[pl.ds(c, 1), :] = folded(dot(stacked(force[c]), patch[c]), 16, MEMBERS)[:1] * jnp.concatenate([scale, scale], axis=1)
+
+
+def apply(fields, weight, picked, turns, norms, shares, nudges, analysed):
+    columns = range(COLS)
+    x = []
+    for c in columns:
+        parts = [fields[pl.ds((m * 4 + var) * 16 + c, 8, stride=128), :] for m in range(2) for var in range(4)]
+        x.append(jnp.concatenate([jnp.concatenate(parts[:4], axis=0), jnp.concatenate(parts[4:], axis=0)], axis=1))
+    mean = [jnp.sum(a, axis=1, keepdims=True) * (1.0 / MEMBERS) for a in x]
+    pert = [a - b for a, b in zip(x, mean)]
+    patch = [patch_of(picked, c) for c in columns]
+    cross = []
+    for c in columns:
+        p = jnp.concatenate([patch[c][:, :MEMBERS], patch[c][:, MEMBERS:]], axis=0)
+        scale = weight[pl.ds(c, 1), :] * norms[pl.ds(c, 1), :] * (1.0 / (MEMBERS - 1.0))
+        cross.append(folded(dot_t(stacked(pert[c]), p), ROWS, PATCH) * scale)
+    u = [folded(dot(stacked(cross[c]), patch_of(turns, c)), ROWS, PATCH) for c in columns]
+    spread = [folded(dot(stacked(u[c]), patch[c]), ROWS, MEMBERS) for c in columns]
+    for c in columns:
+        scale, share = jnp.sqrt(norms[pl.ds(c, 1), :]), shares[pl.ds(c, 1), :]
+        scale, share = jnp.concatenate([scale, scale], axis=1), jnp.concatenate([share, share], axis=1)
+        moved = (share * pert[c] + spread[c]) * scale
+        out = moved + (mean[c] + jnp.sum(moved * nudges[pl.ds(c, 1), :], axis=1, keepdims=True) * (1.0 / (MEMBERS - 1.0)))
+        for m in range(2):
+            for var in range(4):
+                analysed[pl.ds((m * 4 + var) * 16 + c, 8, stride=128), :] = out[var * 8:var * 8 + 8, m * 128:m * 128 + 128]
 
 
 def turn_members(src, dst):
@@ -528,8 +516,8 @@
 
 def kernel(state_in, branch_in, site_in, value_in, index_in, weight_in, result,
            state, branch, site, value, weight, stab, stab_edge, to_next, to_prev, from_prev, from_next, mixed, edge, tiles, columns, obs, table,
-           index, fields, lookup, turned, gap, analysed, picked, steps, turns, norms, outgoing, landed, placed,
-           halo_send, halo_recv, send_sems, plane_sems, x_sems, core_sem, out_sems, in_sems, load_sems, store_sems, arrived):
+           index, fields, lookup, turned, gap, analysed, picked, shares, turns, norms, nudges, outgoing, landed, placed, sites_at, parts, chosen,
+           halo_send, halo_recv, send_sems, plane_sems, x_sems, core_sem, out_sems, in_sems, back_sems, load_sems, store_sems, arrived):
     me, tile = lax.axis_index("mem"), lax.axis_index("tile")
     greeting = greet(me, tile)
     next(greeting)
@@ -543,74 +531,82 @@
     def state_here():
         loads[0].wait()
         loads[1].wait()
+
+    def meanwhile():
+        for load in loads[3:]:
+            load.wait()
+        mark_sites(site, sites_at)
+        mark_patch(index, weight, turned, chosen)
     rounds = pass_on(arrived, me, tile)
     forecast_body(state, branch, stab, stab_edge, to_next, to_prev, from_prev, from_next, mixed, edge, halo_send, halo_recv, me, tile,
-                  greeting, rounds, state_here, loads[2].wait)
-    for load in loads[3:]:
-        load.wait()
+                  greeting, rounds, state_here, loads[2].wait, meanwhile)
     slot = slot_of(me)
     here = pl.ds(pl.multiple_of(slot * 8, 8), 8)
 
-    def send_columns():
-        def to_owner(to):
-            send(tiles.at[pl.ds(pl.multiple_of(to * 8, 8), 8)], columns.at[here], out_sems.at[0], in_sems.at[0], to, tile)
-        each_device(me, to_owner)
-        columns[here, :] = tiles[pl.ds(pl.multiple_of(me * 8, 8), 8), :]
-
-    observe(mixed, site, obs)
+    def to_owner(to):
+        send(tiles.at[pl.ds(pl.multiple_of(to * 8, 8), 8)], columns.at[here], out_sems.at[0], in_sems.at[0], to, tile)
+    observe(mixed, site, sites_at, parts, obs)
     table[pl.ds(pl.multiple_of(slot * 16, 16), 16), :] = obs[...]
     gather = gather_obs(table, send_sems, plane_sems, x_sems, core_sem, me, tile)
     next(gather)
     cut_columns(mixed, tiles)
     for _ in rounds:
         pass
-    if ORDER == 0:
-        send_columns()
-        next(gather)
-    else:
-        next(gather)
-        send_columns()
+    next(gather)
+    each_device(me, to_owner)
+    columns[here, :] = tiles[pl.ds(pl.multiple_of(me * 8, 8), 8), :]
     for _ in gather:
         pass
-    prepare(table, value, index, weight, lookup, turned, gap)
-    pick_obs(turned, lookup, picked)
-    sweep(turned, weight, picked, steps, turns, norms)
+    prepare(table, value, index, lookup, gap)
+    pick_obs(chosen, lookup, picked)
+    sweep(turned, weight, gap, picked, turns, norms, shares, nudges)
     wait_rows(tiles, out_sems.at[0], 8 * (MEM - 1))
     wait_rows(columns, in_sems.at[0], 8 * (MEM - 1))
     turn_members(columns, fields)
-    apply(fields, weight, gap, picked, steps, turns, norms, analysed)
+    apply(fields, weight, picked, turns, norms, shares, nudges, analysed)
     turn_back(analysed, outgoing)
     mine = pl.ds(pl.multiple_of(me * 8, 8), 8)
 
     def give_back(to):
-        send(outgoing.at[pl.ds(pl.multiple_of(slot_of(to) * 8, 8), 8)], landed.at[mine], out_sems.at[1], in_sems.at[1], to, tile)
+        send(outgoing.at[pl.ds(pl.multiple_of(slot_of(to) * 8, 8), 8)], landed.at[mine], out_sems.at[1], back_sems.at[div(me, 8)], to, tile)
     each_device(me, give_back)
-    landed[mine, :] = outgoing[here, :]
+    pltpu.make_async_copy(outgoing.at[here], landed.at[mine], back_sems.at[div(me, 8)]).start()
+    whole = placed.reshape(4, ROWS, 8, LANES)
+    stores = []
+    for i in range(1, 5):
+        lt = rem(div(me, 8) + i, 4)
+        for x in range(4):
+            wait_rows(landed, back_sems.at[x * 4 + lt], 64)
+        for x in range(4):
+            place(landed, placed, x, lt)
+        for m in range(2):
+            lanes = pl.ds(pl.multiple_of(lt * LANES, LANES), LANES)
+            stores.append(pltpu.make_async_copy(whole.at[lt, :, pl.ds(m * 4, 4)], result.at[:, m, :, lanes], store_sems.at[i * 2 - 2 + m]))
+            stores[-1].start()
     wait_rows(outgoing, out_sems.at[1], 8 * (MEM - 1))
-    wait_rows(landed, in_sems.at[1], 8 * (MEM - 1))
-    place(landed, placed)
-    whole = placed.reshape(4, ROWS, 8, LANES)
-    stores = [pltpu.make_async_copy(whole.at[lt, :, pl.ds(m * 4, 4)], result.at[:, m, :, pl.ds(lt * LANES, LANES)], store_sems.at[lt * 2 + m])
-              for lt in range(4) for m in range(2)]
-    for store in stores:
-        store.start()
     for store in stores:
         store.wait()
 
 
-ORDER = 1
-
-
-def place(landed, result):
-    def body(n, carry):
-        x, lt = div(n, 4), rem(n, 4)
-        blocks = [landed[pl.ds(pl.multiple_of((x * 32 + lt * 8 + g) * 8, 8), 8), :] for g in range(8)]
-        blocks = block_transpose(blocks)
-        for m in range(2):
-            for var in range(4):
-                result[pl.ds(lt * 256 + var * 64 + m * 4 + x, 8, stride=8), :] = blocks[m * 4 + var]
-        return carry
-    lax.fori_loop(0, 16, body, 0, unroll=4)
+def copy_kernel(source, result, held, sems):
+    parts = [pl.ds(n * 8, 8) for n in range(4)]
+    reads = [pltpu.make_async_copy(source.at[p], held.at[p], sems.at[n]) for n, p in enumerate(parts)]
+    writes = [pltpu.make_async_copy(held.at[p], result.at[p], sems.at[4 + n]) for n, p in enumerate(parts)]
+    for read in reads:
+        read.start()
+    for read, write in zip(reads, writes):
+        read.wait()
+        write.start()
+    for write in writes:
+        write.wait()
+
+
+def place(landed, result, x, lt):
+    blocks = [landed[pl.ds(pl.multiple_of((x * 32 + lt * 8 + g) * 8, 8), 8), :] for g in range(8)]
+    blocks = block_transpose(blocks)
+    for m in range(2):
+        for var in range(4):
+            result[pl.ds(lt * 256 + var * 64 + m * 4 + x, 8, stride=8), :] = blocks[m * 4 + var]
 
 
 def shape(*dims, dtype=F32):
@@ -634,12 +630,22 @@
             rows(64), rows(64), rows(128, WIDTH), rows(128, WIDTH), rows(128, WIDTH), rows(128, WIDTH),
             rows(1024), rows(1024), rows(1024), rows(1024), rows(16), rows(MEM * 16),
             rows(COLS, LANES, jnp.int32), rows(1024), rows(OBS, 2 * MEMBERS, BF16), rows(LANES), rows(COLS), rows(1024),
-            rows(COLS * PATCH, 2 * MEMBERS, BF16), rows(COLS * PATCH, 2 * PATCH, BF16), rows(COLS * PATCH, 2 * PATCH, BF16),
-            rows(COLS), rows(1024), rows(1024), rows(1024),
-            dma((2,)), dma((8,)), dma((3,)), dma((15,)), dma((3,)), dma(()), dma((2,)), dma((2,)), dma((7,)), dma((8,)), regular((3,)),
+            rows(COLS * PATCH, 2 * MEMBERS, BF16), rows(COLS), rows(COLS * PATCH, 2 * PATCH, BF16),
+            rows(COLS), rows(COLS, MEMBERS), rows(1024), rows(1024), rows(1024),
+            rows(2048, OBS, BF16), rows(192, 2048, BF16), rows(COLS * PATCH, OBS, BF16),
+            dma((2,)), dma((8,)), dma((3,)), dma((15,)), dma((3,)), dma(()), dma((2,)), dma((1,)), dma((16,)), dma((7,)), dma((8,)), regular((3,)),
         ],
         compiler_params=pltpu.CompilerParams(collective_id=1, has_side_effects=True, vmem_limit_bytes=60 * 1024 * 1024),
     )(state.reshape(ROWS, 2, 4, WIDTH), branch, obs_site.reshape(8, LANES), obs_value.reshape(8, LANES), patch_index, patch_weight.reshape(COLS, LANES))
+    result = pl.pallas_call(
+        copy_kernel,
+        name="copy_out",
+        out_shape=shape(ROWS, 2, 4, WIDTH),
+        in_specs=[HBM],
+        out_specs=HBM,
+        scratch_shapes=[pltpu.VMEM((ROWS, 2, 4, WIDTH), F32), dma((8,))],
+        compiler_params=pltpu.CompilerParams(vmem_limit_bytes=60 * 1024 * 1024),
+    )(result)
     return result.reshape(state.shape)
 
 

time: 84.7 us -> 77.7 us (0.917)
  Pallas kernels: 82.7 us -> 77.5 us
  local copies, waits for them, and re-layouts: 1.87 us -> 0 us
    pallas_call x1, Pallas kernels: 82.7 us -> 75.7 us  [per_device(): pl.pallas_call(kernel, name='forecast_analysis', out_shape=shape(ROWS, 2,...]
    unnamed x1 -> x0, local copies, waits for them, and re-layouts: 1.87 us -> none
    pallas_call x0 -> x1, Pallas kernels: none -> 1.82 us  [per_device(): pl.pallas_call(copy_kernel, name='copy_out', out_shape=shape(ROWS, 2, 4,...]
where the time goes in v3:
time: 77.7 us; the launch traced here: 77.5 us
  Pallas kernels  77.5 us (100%)
    pallas_call x1, Pallas kernels, per_device(): pl.pallas_call(kernel, name='forecast_analysis', out_shape=shape(ROWS, 2,...  75.7 us
    pallas_call x1, Pallas kernels, per_device(): pl.pallas_call(copy_kernel, name='copy_out', out_shape=shape(ROWS, 2, 4,...  1.82 us

profile of v3, /device:TPU:1, one launch (start us, length us, event | category | flops | bytes accessed | tf_op | source)
XLA Modules:
  0.0 77.5 jit_solution(14201074468619822791)
XLA Ops:
  0.0 75.7 %forecast_analysis.1.source = f32[32,2,4,512]{3,2,1,0:T(4,128)} custom-call(f32[32,2,4,512]{3,2,1,0:T(4,128)} %bitcast.5, s32[16,512]{1,0:T(8,128)} %branch_in.1, s32[8,128]{1,0:T(8,128)} %bitcast.7, f32[8,128]{1,0:T(8,128)} %bitcast.8, s32[1,2048,128]{2,1,0:T(8,128)} %index_in.1, f32[16,128]{1,0:T(8,128)} %bitcast.6), custom_call_target="tpu_custom_call" | custom-call | tf_op jit(solution)/shard_map/forecast_analysis/pallas_call | solution.py:622
  75.7 1.8 %copy_out.1 = f32[32,2,4,512]{3,2,1,0:T(4,128)} custom-call(f32[32,2,4,512]{3,2,1,0:T(4,128)} %forecast_analysis.1.source), custom_call_target="tpu_custom_call" | custom-call | tf_op jit(solution)/shard_map/copy_out/pallas_call | solution.py:640

commit v4 on v3

--- a/solution.py
+++ b/solution.py
@@ -117,16 +117,17 @@
     return m, h
 
 
-def mix_columns(src, dst, stab_ref):
+def mix_columns(*sets):
     def body(lt, carry):
-        base = pl.multiple_of(lt * 256, 256)
-        field = [[src[pl.ds(base + (var * 8 + k) * 8, 8), :] for k in range(LEVELS)] for var in range(4)]
-        sbase = pl.multiple_of(lt * 16, 16)
-        stab_m, stab_h = stab_ref[pl.ds(sbase, 8), :], stab_ref[pl.ds(sbase + 8, 8), :]
-        new = column_step(*field, stab_m, stab_h)
-        for var in range(4):
-            for k in range(LEVELS):
-                dst[pl.ds(base + (var * 8 + k) * 8, 8), :] = new[var][k]
+        base, sbase = pl.multiple_of(lt * 256, 256), pl.multiple_of(lt * 16, 16)
+        new = []
+        for ref, stab in sets:
+            field = [[ref[pl.ds(base + (var * 8 + k) * 8, 8), :] for k in range(LEVELS)] for var in range(4)]
+            new.append(column_step(*field, stab[pl.ds(sbase, 8), :], stab[pl.ds(sbase + 8, 8), :]))
+        for (ref, stab), values in zip(sets, new):
+            for var in range(4):
+                for k in range(LEVELS):
+                    ref[pl.ds(base + (var * 8 + k) * 8, 8), :] = values[var][k]
         return carry
     lax.fori_loop(0, 4, body, 0)
 
@@ -202,8 +203,7 @@
         wait_rows(from_prev, halo_recv.at[var], 32)
         wait_rows(from_next, halo_recv.at[4 + var], 32)
         lax.fori_loop(var * 8, var * 8 + 8, first, 0, unroll=8)
-    mix_columns(mixed, mixed, stab)
-    mix_columns(edge, edge, stab_edge)
+    mix_columns((mixed, stab), (edge, stab_edge))
     next(rounds)
 
     def second(row, carry):
@@ -215,7 +215,7 @@
         put_tiles(mixed, row, laplace_step(centre, up, down))
         return carry
     lax.fori_loop(0, ROWS, second, 0, unroll=8)
-    mix_columns(mixed, mixed, stab)
+    mix_columns((mixed, stab))
     wait_rows(to_next, halo_send.at[0], 128)
     wait_rows(to_prev, halo_send.at[1], 128)
 
@@ -307,13 +307,15 @@
         wait_rows(table, x_sems.at[j - 1], 256)
         plane = part(core * 64 + rem(x + 4 - j, 4) * 16, 16)
         send(plane, plane, send_sems.at[2], core_sem, device_at(1 - core, x, y, z), tile)
+    yield
     wait_rows(table, core_sem, 1024)
+    yield
     wait_rows(table, send_sems.at[0], 16 * 15)
     wait_rows(table, send_sems.at[1], 256 * 3)
     wait_rows(table, send_sems.at[2], 1024)
 
 
-def each_device(me, do):
+def each_device(me, do, far=True, close=True):
     core, y, z, x = rem(me, 2), rem(div(me, 2), 8), rem(div(me, 16), 2), div(me, 32)
 
     def all_at(y_to, z_to, own):
@@ -329,9 +331,11 @@
             all_at(rem(y + step, 8), z_to, False)
             return carry
         return one
-    lax.fori_loop(0, 8, body(1 - z), 0)
-    lax.fori_loop(0, 7, body(z), 0)
-    all_at(y, z, True)
+    if far:
+        lax.fori_loop(0, 8, body(1 - z), 0)
+    if close:
+        lax.fori_loop(0, 7, body(z), 0)
+        all_at(y, z, True)
 
 
 def near(me):
@@ -462,9 +466,9 @@
     second = times([2.25 * one - 1.5 * m + 0.25 * q for m, q in zip(turn, turn_square)], turn_wide)
     f0, f1 = [1.5 - 0.5 * r for r in t], [1.5 - 0.5 * r for r in t1]
     f2 = [1.5 - 0.5 * r * c_rate(r) for r in t1]
-    left = times([1.5 * one - 0.5 * m + a * b for m, a, b in zip(turn, f0, h_k)], [beside(1.5 * one - 0.5 * m) for m in second])
-    right = times([a * b * m for a, b, m in zip(f0, f1, h_k)], [beside(h(r, m, q)) for r, m, q in zip(t1, turn, turn_square)])
-    wide = [beside(-0.5 * (a + b)) for a, b in zip(left, right)]
+    left = [jnp.concatenate([stacked(1.5 * one - 0.5 * m + a * b), stacked(a * c * b)], axis=1) for m, a, c, b in zip(turn, f0, f1, h_k)]
+    right = [jnp.concatenate([beside(1.5 * one - 0.5 * m), beside(h(r, y, q))], axis=0) for m, r, y, q in zip(second, t1, turn, turn_square)]
+    wide = [beside(-0.5 * folded(dot(a, b), PATCH, PATCH)) for a, b in zip(left, right)]
     first_row = lax.broadcasted_iota(jnp.int32, (16, PATCH), 0) == 0
     force = [jnp.where(first_row, weight[pl.ds(c, 1), :] * gap[pl.ds(c, 1), :], 0.0) for c in columns]
     share = [a * b * c for a, b, c in zip(f0, f1, f2)]
@@ -555,11 +559,13 @@
     next(gather)
     each_device(me, to_owner)
     columns[here, :] = tiles[pl.ds(pl.multiple_of(me * 8, 8), 8), :]
-    for _ in gather:
-        pass
+    next(gather)
+    next(gather)
     prepare(table, value, index, lookup, gap)
     pick_obs(chosen, lookup, picked)
     sweep(turned, weight, gap, picked, turns, norms, shares, nudges)
+    for _ in gather:
+        pass
     wait_rows(tiles, out_sems.at[0], 8 * (MEM - 1))
     wait_rows(columns, in_sems.at[0], 8 * (MEM - 1))
     turn_members(columns, fields)

time: 77.7 us -> 77.3 us (level)
  no operation moved by 1% of the time
where the time goes in v4:
time: 77.3 us; the launch traced here: 76.8 us
  Pallas kernels  76.8 us (99%)
    pallas_call x1, Pallas kernels, per_device(): pl.pallas_call(kernel, name='forecast_analysis', out_shape=shape(ROWS, 2,...  75 us
    pallas_call x1, Pallas kernels, per_device(): pl.pallas_call(copy_kernel, name='copy_out', out_shape=shape(ROWS, 2, 4,...  1.82 us

profile of v4, /device:TPU:1, one launch (start us, length us, event | category | flops | bytes accessed | tf_op | source)
XLA Modules:
  0.0 76.8 jit_solution(2569717639640929387)
XLA Ops:
  0.0 75.0 %forecast_analysis.1.source = f32[32,2,4,512]{3,2,1,0:T(4,128)} custom-call(f32[32,2,4,512]{3,2,1,0:T(4,128)} %bitcast.5, s32[16,512]{1,0:T(8,128)} %branch_in.1, s32[8,128]{1,0:T(8,128)} %bitcast.7, f32[8,128]{1,0:T(8,128)} %bitcast.8, s32[1,2048,128]{2,1,0:T(8,128)} %index_in.1, f32[16,128]{1,0:T(8,128)} %bitcast.6), custom_call_target="tpu_custom_call" | custom-call | tf_op jit(solution)/shard_map/forecast_analysis/pallas_call | solution.py:628
  75.0 1.8 %copy_out.1 = f32[32,2,4,512]{3,2,1,0:T(4,128)} custom-call(f32[32,2,4,512]{3,2,1,0:T(4,128)} %forecast_analysis.1.source), custom_call_target="tpu_custom_call" | custom-call | tf_op jit(solution)/shard_map/copy_out/pallas_call | solution.py:646
